TPU v7x, 256 devices: a whole 4x4x8 slice. The times are simulated.
256 devices in a mesh: paper: 64 (over z, y, core), author: 4 (over x).
Axes of the slice: x: 4, y: 4, z: 8, core: 2. Of those that a mesh axis runs over, the one named last changes fastest.
Arguments:
- paper_feat: bfloat16 [16384, 1024], P('paper', 'author'), may hold values from -6 to 6
- author_feat: bfloat16 [16384, 1024], P('paper', 'author'), may hold values from -6 to 6
- cite_owner: int32 [3072, 1], P('paper'), may hold values from 0 to 63; in each aligned block of 48 rows (0 to 47, 48 to 95, ...) no two rows name the same one
- cite_source: int32 [3072], P('paper'), may hold values from 0 to 1
- cite_target: int32 [3072], P('paper'), may hold values from 0 to 1
- cite_edges: int32 [3072], P('paper'), may hold values from 8 to 64
- cite_count: int32 [64], P('paper'), may hold values from 36 to 48, as said below
- citation_weight_tiles: bfloat16 [3072, 128, 128], P('paper'), may hold values from 0 to 1
- write_owner: int32 [2048, 1], P('paper'), may hold values from 0 to 63; in each aligned block of 32 rows (0 to 31, 32 to 63, ...) no two rows name the same one
- write_paper: int32 [2048], P('paper'), may hold values from 0 to 1
- write_author: int32 [2048], P('paper'), may hold values from 0 to 1
- write_edges: int32 [2048], P('paper'), may hold values from 8 to 64
- authorship_weight_tiles: bfloat16 [2048, 128, 128], P('paper'), may hold values from 0 to 1
- w_self: bfloat16 [1024, 1024], replicated, may hold values from -0.1875 to 0.1875
- w_cite: bfloat16 [1024, 1024], replicated, may hold values from -0.1875 to 0.1875
- w_write: bfloat16 [1024, 1024], replicated, may hold values from -0.1875 to 0.1875
- cotangent: bfloat16 [16384, 1024], P('paper', 'author'), may hold values from -6 to 6
Outputs:
- paper_out: bfloat16 [16384, 1024], P('paper', 'author')
- paper_grad: bfloat16 [16384, 1024], P('paper', 'author')
- author_grad: bfloat16 [16384, 1024], P('paper', 'author')
Inputs may be any that keep to these rules, and one draw needn't show every extreme that they name: `cite_owner`: among the 48 tiles of one paper index (live or not), at most 1 have their source on any one paper index. The live tiles of a paper index are the first cite_count of its list; some paper index has all 48 live. `write_owner`: among the 32 tiles of one paper index, at most 1 take their author block from any one paper index.
All inputs are finite; a program needn't handle non-finite values.
Results may differ from a plain program's by a relative error of at most 0.007.
Values may be sent and summed in bfloat16 or wider, within the bound.
A program may use at most 128 MiB of HBM per device.

v0:
```python
import jax
import jax.numpy as jnp
from jax import lax
from jax.sharding import PartitionSpec as P

TOP_PRECISION = lax.Precision.HIGHEST


def silu_slope(values):
    sigma = jax.nn.sigmoid(values)
    return sigma * (1.0 + values * (1.0 - sigma))


def matmul(left, right):
    return jnp.dot(left, right, preferred_element_type=jnp.float32)


def matmul_flipped(left, right):
    return lax.dot_general(
        left, right, (((1,), (1,)), ((), ())), preferred_element_type=jnp.float32
    )


def slot_layout(owners, slot_count, slot_total):
    count = owners.shape[0]
    order = jnp.arange(count, dtype=jnp.int32)
    earlier = (owners[:, None] == owners[None, :]) & (order[:, None] > order[None, :])
    rank = jnp.sum(earlier.astype(jnp.int32), axis=1)
    position = owners * slot_count + rank
    positioned_rows = position[:, None] == jnp.arange(slot_total, dtype=jnp.int32)[None, :]
    return (position, positioned_rows)


def body(
    paper_feat,
    author_feat,
    cite_owner,
    cite_source,
    cite_target,
    cite_edges,
    cite_count,
    citation_weight_tiles,
    write_owner,
    write_paper,
    write_author,
    write_edges,
    authorship_weight_tiles,
    w_self,
    w_cite,
    w_write,
    cotangent,
):
    peer_count = lax.axis_size("paper")
    tile_total = citation_weight_tiles.shape[0]
    tile_rows = citation_weight_tiles.shape[1]
    paper_rows, quarter = paper_feat.shape
    author_rows = author_feat.shape[0]
    paper_blocks = paper_rows // tile_rows
    author_blocks = author_rows // tile_rows
    slot_count = tile_total // peer_count + 1
    slot_total = peer_count * slot_count
    write_total = authorship_weight_tiles.shape[0]
    wslot_count = write_total // peer_count + 1
    wslot_total = peer_count * wslot_count
    block_range = jnp.arange(paper_blocks, dtype=jnp.int32)
    author_range = jnp.arange(author_blocks, dtype=jnp.int32)
    position, positioned_rows = slot_layout(cite_owner[:, 0], slot_count, slot_total)
    tile_order = jnp.arange(tile_total, dtype=jnp.int32)
    wanted = jnp.sum(jnp.where(positioned_rows, cite_source[:, None], 0), axis=0)
    incoming_ids = lax.all_to_all(
        wanted.reshape(peer_count, slot_count), "paper", split_axis=0, concat_axis=0, tiled=True
    )
    live_tile = tile_order < cite_count[0]
    tile_scale = jnp.where(live_tile, 1.0 / cite_edges.astype(jnp.float32), 0.0)
    target_hot = jnp.where(cite_target[:, None] == block_range[None, :], tile_scale[:, None], 0.0)
    slotted_weight_tiles = jnp.einsum(
        "tk,tab->kab",
        positioned_rows.astype(jnp.bfloat16),
        citation_weight_tiles,
        preferred_element_type=jnp.float32,
    ).astype(jnp.bfloat16)
    slotted_target_index = jnp.einsum(
        "tk,tp->kp", positioned_rows.astype(jnp.float32), target_hot, precision=TOP_PRECISION
    )
    pieces = lax.all_gather(paper_feat, "paper", axis=0, tiled=True)
    shard_count = pieces.shape[0] // paper_rows
    span = shard_count * slot_count
    shard_of = jnp.arange(span, dtype=jnp.int32) // slot_count
    stacked = pieces.reshape(shard_count * paper_blocks, tile_rows, quarter)
    selected_rows = jnp.take(stacked, shard_of * paper_blocks + wanted, axis=0)
    partial_block_value = jnp.einsum(
        "eih,ehp->eip", slotted_weight_tiles, selected_rows, preferred_element_type=jnp.float32
    )
    citation_accumulator = jnp.einsum(
        "nr,nmh->rmh", slotted_target_index, partial_block_value, precision=TOP_PRECISION
    )
    cite_sum = citation_accumulator.reshape(paper_rows, quarter).astype(jnp.bfloat16)
    wposition, wplaced = slot_layout(write_owner[:, 0], wslot_count, wslot_total)
    wanted_authors = jnp.sum(jnp.where(wplaced, write_author[:, None], 0), axis=0)
    author_ids = lax.all_to_all(
        wanted_authors.reshape(peer_count, wslot_count),
        "paper",
        split_axis=0,
        concat_axis=0,
        tiled=True,
    )
    author_stack = author_feat.reshape(author_blocks, tile_rows, quarter)
    author_out = jnp.take(author_stack, author_ids.reshape(-1), axis=0).reshape(
        peer_count, wslot_count, tile_rows, quarter
    )
    author_in = lax.all_to_all(author_out, "paper", split_axis=0, concat_axis=0, tiled=True)
    write_scale = 1.0 / write_edges.astype(jnp.float32)
    authorship_sources = jnp.take(
        author_in.reshape(wslot_total, tile_rows, quarter), wposition, axis=0
    )
    authorship_products = jnp.einsum(
        "eih,ehp->eip",
        authorship_weight_tiles,
        authorship_sources,
        preferred_element_type=jnp.float32,
    )
    paper_onehot_mask = jnp.where(
        write_paper[:, None] == block_range[None, :], write_scale[:, None], 0.0
    )
    authorship_sum = jnp.einsum(
        "nr,nmh->rmh", paper_onehot_mask, authorship_products, precision=TOP_PRECISION
    )
    authorship_sum = authorship_sum.reshape(paper_rows, quarter).astype(jnp.bfloat16)
    column = lax.axis_index("author") * quarter
    feats = lax.all_gather(paper_feat, "author", axis=1, tiled=True)
    cites = lax.all_gather(cite_sum, "author", axis=1, tiled=True)
    writes = lax.all_gather(authorship_sum, "author", axis=1, tiled=True)
    span = feats.shape[1]

    def window(weight):
        return lax.dynamic_slice(weight, (0, column), (span, quarter))

    preact = (
        matmul(feats, window(w_self))
        + matmul(cites, window(w_cite))
        + matmul(writes, window(w_write))
    )
    paper_out = (paper_feat.astype(jnp.float32) + jax.nn.silu(preact)).astype(jnp.bfloat16)
    grad_pre = (cotangent.astype(jnp.float32) * silu_slope(preact)).astype(jnp.bfloat16)
    pieces = lax.all_gather(grad_pre, "author", axis=1, tiled=True)
    fold_span = pieces.shape[1]

    def flipped(weight):
        return matmul_flipped(pieces, lax.dynamic_slice(weight, (column, 0), (quarter, fold_span)))

    self_back = flipped(w_self)
    cite_back = flipped(w_cite)
    write_back = flipped(w_write)
    cite_grad = cite_back.astype(jnp.bfloat16).reshape(paper_blocks, tile_rows, quarter)
    target_indices = jnp.take(cite_grad, cite_target, axis=0)
    returned_rows = jnp.einsum(
        "pdg,pdw->pgw", citation_weight_tiles, target_indices, preferred_element_type=jnp.float32
    )
    returned_rows = (returned_rows * tile_scale[:, None, None]).astype(jnp.bfloat16)
    outgoing_grad = jnp.einsum(
        "hs,hip->sip",
        positioned_rows.astype(jnp.bfloat16),
        returned_rows,
        preferred_element_type=jnp.float32,
    )
    outgoing_grad = outgoing_grad.astype(jnp.bfloat16).reshape(
        peer_count, slot_count, tile_rows, quarter
    )
    arrived = lax.all_to_all(outgoing_grad, "paper", split_axis=0, concat_axis=0, tiled=True)
    arrived_hot = (incoming_ids.reshape(-1)[:, None] == block_range[None, :]).astype(jnp.bfloat16)
    cite_return = jnp.einsum(
        "kp,kac->pac",
        arrived_hot,
        arrived.reshape(slot_total, tile_rows, quarter),
        preferred_element_type=jnp.float32,
    )
    paper_grad = (
        cotangent.astype(jnp.float32) + self_back + cite_return.reshape(paper_rows, quarter)
    ).astype(jnp.bfloat16)
    write_grad = write_back.astype(jnp.bfloat16).reshape(paper_blocks, tile_rows, quarter)
    authorship_targets = jnp.take(write_grad, write_paper, axis=0)
    author_products = jnp.einsum(
        "pdg,pdw->pgw",
        authorship_weight_tiles,
        authorship_targets,
        preferred_element_type=jnp.float32,
    )
    author_products = (author_products * write_scale[:, None, None]).astype(jnp.bfloat16)
    author_send = jnp.einsum(
        "hs,hip->sip",
        wplaced.astype(jnp.bfloat16),
        author_products,
        preferred_element_type=jnp.float32,
    )
    author_send = author_send.astype(jnp.bfloat16).reshape(
        peer_count, wslot_count, tile_rows, quarter
    )
    author_back = lax.all_to_all(author_send, "paper", split_axis=0, concat_axis=0, tiled=True)
    author_hot = (author_ids.reshape(-1)[:, None] == author_range[None, :]).astype(jnp.bfloat16)
    author_grad = jnp.einsum(
        "kp,kac->pac",
        author_hot,
        author_back.reshape(wslot_total, tile_rows, quarter),
        preferred_element_type=jnp.float32,
    )
    author_grad = author_grad.reshape(author_rows, quarter).astype(jnp.bfloat16)
    return (paper_out, paper_grad, author_grad)


def solution(mesh):
    in_specs = (
        P("paper", "author"),
        P("paper", "author"),
        P("paper", None),
        P("paper"),
        P("paper"),
        P("paper"),
        P("paper"),
        P("paper", None, None),
        P("paper", None),
        P("paper"),
        P("paper"),
        P("paper"),
        P("paper", None, None),
        P(),
        P(),
        P(),
        P("paper", "author"),
    )
    out_specs = (P("paper", "author"), P("paper", "author"), P("paper", "author"))
    return jax.shard_map(body, mesh=mesh, in_specs=in_specs, out_specs=out_specs, check_vma=False)
```

profile of v0, /device:TPU:1, one launch (start us, length us, event | category | flops | bytes accessed | tf_op | source)
XLA Modules:
  0.0 489.8 jit_solution(11593306411064109347)
XLA Ops:
  10.3 22.3 %all_to_all.39 = s32[64,1,1]{2,1,0:T(1,128)S(1)} all-to-all(s32[64,1,1]{2,1,0:T(1,128)S(1)} %copy.96), channel_id=1, replica_groups=mesh['paper'=64,'author'=4] {'paper'}, dimensions={0} | all-to-all | bytes 512 | tf_op jit(solution)/shard_map/all_to_all | solution.py:100
  36.7 4.6 bitcast_select_fusion
  41.3 5.9 %all-to-all-start.1 = ((bf16[64,1,128,256]{3,2,1,0:T(8,128)(2,1)}), bf16[64,1,128,256]{3,2,1,0:T(8,128)(2,1)}, u32[]{:S(2)}, u32[]{:S(2)}) async-start(bf16[64,1,128,256]{3,2,1,0:T(8,128)(2,1)} %bitcast_select_fusion), calls=%async_computation.1 | async-start | bytes 8388608 | tf_op jit(solution)/shard_map/all_to_all | solution.py:111
  49.7 11.6 %all_gather.15 = bf16[256,1024]{1,0:T(8,128)(2,1)S(1)} all-gather(bf16[256,256]{1,0:T(8,128)(2,1)S(1)} %copy-done.2), channel_id=1, replica_groups=mesh['paper'=64,'author'=4] {'author'}, dimensions={1}, use_global_device_ids=true | all-gather | bytes 655360 | tf_op jit(solution)/shard_map/all_gather | solution.py:130
  66.1 96.1 %all-to-all-done.1 = bf16[64,1,128,256]{3,2,1,0:T(8,128)(2,1)} async-done(((bf16[64,1,128,256]{3,2,1,0:T(8,128)(2,1)}), bf16[64,1,128,256]{3,2,1,0:T(8,128)(2,1)}, u32[]{:S(2)}, u32[]{:S(2)}) %all-to-all-start.1) | async-done | bytes 4194336 | tf_op jit(solution)/shard_map/all_to_all | solution.py:111
  162.2 6.8 %all-to-all-start.2 = ((s32[64,1,1]{2,1,0:T(1,128)}), s32[64,1,1]{2,1,0:T(1,128)}, u32[]{:S(2)}, u32[]{:S(2)}) async-start(s32[64,1,1]{2,1,0:T(1,128)} %copy.103), calls=%async_computation.2 | async-start | bytes 65536 | tf_op jit(solution)/shard_map/all_to_all | solution.py:70
  173.2 4.6 convolution_bitcast_fusion
  177.9 5.5 %copy.98 = f32[32,128,256]{2,0,1:T(8,128)} copy(f32[32,128,256]{1,2,0:T(8,128)} %convolution_bitcast_fusion) | data formatting | bytes 8388608 | tf_op jit(solution)/shard_map/eih,ehp->eip/dot_general | solution.py:116
  187.7 11.5 %all_gather.18 = bf16[256,1024]{1,0:T(8,128)(2,1)S(1)} all-gather(bf16[256,256]{1,0:T(8,128)(2,1)S(1)} %bitcast.106), channel_id=1, replica_groups=mesh['paper'=64,'author'=4] {'author'}, dimensions={1}, use_global_device_ids=true | all-gather | bytes 655360 | tf_op jit(solution)/shard_map/all_gather | solution.py:132
  199.2 6.2 %gather_fusion = bf16[64,128,256]{2,1,0:T(8,128)(2,1)} fusion(bf16[128,128,256]{2,1,0:T(8,128)(2,1)} %bitcast.104, s32[1024]{0:T(1024)S(1)} %pad_clamp_fusion.4), kind=kCustom, calls=%fused_computation | custom fusion | bytes 8388864 | tf_op jit(solution)/shard_map/jit(_take)/gather | solution.py:90
  205.3 5.1 %fusion.5 = f32[64,128,256]{2,1,0:T(8,128)S(1)} fusion(bf16[64,128,256]{2,1,0:T(8,128)(2,1)} %gather_fusion, pred[64]{0:T(512)(128)(4,1)S(1)} %compare_and_fusion.3, bf16[64,128,128]{2,0,1:T(8,128)(2,1)} %convolution_convert_fusion), kind=kOutput, calls=%fused_computation.15 | convolution fusion | flops 538968064 | bytes 14680128 | tf_op jit(solution)/shard_map/eih,ehp->eip/dot_general | solution.py:91
  210.4 8.6 %fusion.31 = bf16[2,128,256]{2,0,1:T(2,128)(2,1)S(1)} fusion(f32[64,2,1]{0,1,2:T(2,128)S(1)} %convolution_bitcast_fusion.2, f32[64,128,256]{2,1,0:T(8,128)S(1)} %fusion.5), kind=kOutput, calls=%fused_computation.42 | convolution fusion | flops 50397184 | bytes 8520192 | tf_op jit(solution)/shard_map/nr,nmh->rmh/dot_general | solution.py:94
  219.0 10.1 %all_gather.17 = bf16[256,1024]{1,0:T(8,128)(2,1)S(1)} all-gather(bf16[256,256]{1,0:T(8,128)(2,1)S(1)} %bitcast.107), channel_id=1, replica_groups=mesh['paper'=64,'author'=4] {'author'}, dimensions={1}, use_global_device_ids=true | all-gather | bytes 655360 | tf_op jit(solution)/shard_map/all_gather | solution.py:131
  231.4 9.9 %all_gather.19 = bf16[256,1024]{0,1:T(8,128)(2,1)S(1)} all-gather(bf16[256,256]{0,1:T(8,128)(2,1)S(1)} %get-tuple-element.20), channel_id=1, replica_groups=mesh['paper'=64,'author'=4] {'author'}, dimensions={1}, use_global_device_ids=true | all-gather | bytes 655360 | tf_op jit(solution)/shard_map/all_gather | solution.py:145
  244.2 5.5 %fusion.8 = bf16[48,128,256]{1,2,0:T(8,128)(2,1)} fusion(f32[48]{0:T(128)S(1)} %copy-done.17, bf16[48,128,128]{2,1,0:T(8,128)(2,1)} %param.24, bf16[48,128,256]{2,1,0:T(8,128)(2,1)} %gather_fusion.3, pred[48]{0:T(512)(128)(4,1)S(1)} %copy-done.18), kind=kOutput, calls=%fused_computation.18 | convolution fusion | flops 407371776 | bytes 7864560 | tf_op jit(solution)/shard_map/pdg,pdw->pgw/dot_general | solution.py:156
  249.7 4.9 %copy.105 = bf16[48,128,256]{2,0,1:T(8,128)(2,1)} copy(bf16[48,128,256]{1,2,0:T(8,128)(2,1)} %fusion.8) | data formatting | bytes 6291456 | tf_op jit(solution)/shard_map/convert_element_type | solution.py:159
  257.8 4.4 copy.106
  262.2 18.8 %all-to-all-start.3 = ((bf16[64,1,128,256]{3,2,1,0:T(8,128)(2,1)}), bf16[64,1,128,256]{3,2,1,0:T(8,128)(2,1)}, u32[]{:S(2)}, u32[]{:S(2)}) async-start(bf16[64,1,128,256]{3,2,1,0:T(8,128)(2,1)} %copy.106), calls=%async_computation.3 | async-start | bytes 8388608 | tf_op jit(solution)/shard_map/all_to_all | solution.py:169
  287.7 4.6 copy.110
  299.7 75.5 %all-to-all-done.3 = bf16[64,1,128,256]{3,2,1,0:T(8,128)(2,1)} async-done(((bf16[64,1,128,256]{3,2,1,0:T(8,128)(2,1)}), bf16[64,1,128,256]{3,2,1,0:T(8,128)(2,1)}, u32[]{:S(2)}, u32[]{:S(2)}) %all-to-all-start.3) | async-done | bytes 4194336 | tf_op jit(solution)/shard_map/all_to_all | solution.py:169
  375.2 7.4 %all-to-all-start.4 = ((bf16[64,1,128,256]{3,2,1,0:T(8,128)(2,1)}), bf16[64,1,128,256]{3,2,1,0:T(8,128)(2,1)}, u32[]{:S(2)}, u32[]{:S(2)}) async-start(bf16[64,1,128,256]{3,2,1,0:T(8,128)(2,1)} %copy.111), calls=%async_computation.4 | async-start | bytes 8388608 | tf_op jit(solution)/shard_map/all_to_all | solution.py:198
  385.3 6.5 %copy.121 = bf16[64,128,256]{1,0,2:T(8,128)(2,1)} copy(bf16[64,128,256]{2,1,0:T(8,128)(2,1)} %bitcast.29) | data formatting | bytes 8388608 | tf_op jit(solution)/shard_map/reshape | solution.py:174
  396.8 80.4 %all-to-all-done.4 = bf16[64,1,128,256]{3,2,1,0:T(8,128)(2,1)} async-done(((bf16[64,1,128,256]{3,2,1,0:T(8,128)(2,1)}), bf16[64,1,128,256]{3,2,1,0:T(8,128)(2,1)}, u32[]{:S(2)}, u32[]{:S(2)}) %all-to-all-start.4) | async-done | bytes 4194336 | tf_op jit(solution)/shard_map/all_to_all | solution.py:198
  477.2 4.5 fusion.27
  (93 shorter events, 52.9 us)
Async XLA Ops:
  7.2 223.7 %copy-start = (bf16[1024,1024]{1,0:T(8,128)(2,1)S(1)}, bf16[1024,1024]{1,0:T(8,128)(2,1)}, u32[]{:S(2)}) copy-start(bf16[1024,1024]{1,0:T(8,128)(2,1)} %param.32) | copy-start | bytes 6291460
  7.2 26.7 %copy-start.1 = (bf16[256,256]{1,0:T(8,128)(2,1)S(1)}, bf16[256,256]{1,0:T(8,128)(2,1)}, u32[]{:S(2)}) copy-start(bf16[256,256]{1,0:T(8,128)(2,1)} %param.18) | copy-start | bytes 393220
  7.2 192.0 %all-gather.2.cloned.1.call-start = ((), (), s32[]{:S(2)}) async-start(), calls=%async_computation.5 | async-start | bytes 8519680 | tf_op jit(solution)/shard_map/all_gather | solution.py:85
  9.5 0.7 copy-start.6
  41.2 5.9 %copy-start.2 = (bf16[256,256]{1,0:T(8,128)(2,1)S(1)}, bf16[256,256]{1,0:T(8,128)(2,1)}, u32[]{:S(2)}) copy-start(bf16[256,256]{1,0:T(8,128)(2,1)} %param.17) | copy-start | bytes 393220
  41.2 6.7 %copy-start.4 = (bf16[256,256]{1,0:T(8,128)(2,1)S(1)}, bf16[256,256]{1,0:T(8,128)(2,1)}, u32[]{:S(2)}) copy-start(bf16[256,256]{1,0:T(8,128)(2,1)} %param.33) | copy-start | bytes 393220
  41.2 6.8 %copy-start.11 = (s32[48,1]{0,1:T(1,128)S(1)}, s32[48,1]{0,1:T(1,128)}, u32[]{:S(2)}) copy-start(s32[48,1]{0,1:T(1,128)} %param.19) | copy-start | bytes 580
  41.2 7.0 %copy-start.12 = (s32[48]{0:T(128)S(1)}, s32[48]{0:T(128)}, u32[]{:S(2)}) copy-start(s32[48]{0:T(128)} %param.20) | copy-start | bytes 580
  41.2 7.9 %copy-start.10 = (s32[32,1]{0,1:T(1,128)S(1)}, s32[32,1]{0,1:T(1,128)}, u32[]{:S(2)}) copy-start(s32[32,1]{0,1:T(1,128)} %param.25) | copy-start | bytes 388
  41.3 7.9 %copy-start.14 = (s32[48]{0:T(128)S(1)}, s32[48]{0:T(128)}, u32[]{:S(2)}) copy-start(s32[48]{0:T(128)} %param.21) | copy-start | bytes 580
  41.3 7.9 %copy-start.13 = (s32[48]{0:T(128)S(1)}, s32[48]{0:T(128)}, u32[]{:S(2)}) copy-start(s32[48]{0:T(128)} %param.22) | copy-start | bytes 580
  41.3 20.6 %copy-start.15 = (s32[32]{0:T(128)S(1)}, s32[32]{0:T(128)}, u32[]{:S(2)}) copy-start(s32[32]{0:T(128)} %param.28) | copy-start | bytes 388
  41.3 120.9 %all-to-all-start.1 = ((bf16[64,1,128,256]{3,2,1,0:T(8,128)(2,1)}), bf16[64,1,128,256]{3,2,1,0:T(8,128)(2,1)}, u32[]{:S(2)}, u32[]{:S(2)}) async-start(bf16[64,1,128,256]{3,2,1,0:T(8,128)(2,1)} %bitcast_select_fusion), calls=%async_computation.1 | async-start | bytes 8388608 | tf_op jit(solution)/shard_map/all_to_all | solution.py:111
  49.2 0.5 copy-start.16
  61.9 121.5 %copy-start.8 = (f32[32]{0:T(128)}, f32[32]{0:T(128)S(1)}, u32[]{:S(2)}) copy-start(f32[32]{0:T(128)S(1)} %convert_divide_fusion) | copy-start | bytes 388
  162.2 100.0 %all-to-all-start.2 = ((s32[64,1,1]{2,1,0:T(1,128)}), s32[64,1,1]{2,1,0:T(1,128)}, u32[]{:S(2)}, u32[]{:S(2)}) async-start(s32[64,1,1]{2,1,0:T(1,128)} %copy.103), calls=%async_computation.2 | async-start | bytes 65536 | tf_op jit(solution)/shard_map/all_to_all | solution.py:70
  177.9 5.5 %copy-start.5 = (s32[32]{0:T(128)S(1)}, s32[32]{0:T(128)}, u32[]{:S(2)}) copy-start(s32[32]{0:T(128)} %param.26) | copy-start | bytes 388
  210.4 18.7 %copy-start.3 = (bf16[1024,1024]{1,0:T(8,128)(2,1)S(1)}, bf16[1024,1024]{1,0:T(8,128)(2,1)}, u32[]{:S(2)}) copy-start(bf16[1024,1024]{1,0:T(8,128)(2,1)} %param.31) | copy-start | bytes 6291460
  241.6 2.5 copy-start.17
  241.6 2.5 copy-start.18
  262.2 113.0 %all-to-all-start.3 = ((bf16[64,1,128,256]{3,2,1,0:T(8,128)(2,1)}), bf16[64,1,128,256]{3,2,1,0:T(8,128)(2,1)}, u32[]{:S(2)}, u32[]{:S(2)}) async-start(bf16[64,1,128,256]{3,2,1,0:T(8,128)(2,1)} %copy.106), calls=%async_computation.3 | async-start | bytes 8388608 | tf_op jit(solution)/shard_map/all_to_all | solution.py:169
  281.0 2.5 copy-start.9
  287.7 4.6 copy-start.7
  375.2 102.0 %all-to-all-start.4 = ((bf16[64,1,128,256]{3,2,1,0:T(8,128)(2,1)}), bf16[64,1,128,256]{3,2,1,0:T(8,128)(2,1)}, u32[]{:S(2)}, u32[]{:S(2)}) async-start(bf16[64,1,128,256]{3,2,1,0:T(8,128)(2,1)} %copy.111), calls=%async_computation.4 | async-start | bytes 8388608 | tf_op jit(solution)/shard_map/all_to_all | solution.py:198
Sparse Core Ops, SparseCore 0:
  10.8 134.5 all-gather.1
where the time goes:
time: 499 us; the launch traced here: 490 us
  waiting for transfers between devices  253 us (51%)
  blocking collectives  65.4 us (13%)
  matrix products  54.6 us (11%)
  local copies, waits for them, and re-layouts  51.6 us (10%)
  starting transfers between devices  38.9 us (8%)
  between operations  15.5 us (3%)
  other arithmetic  11 us (2%)
    all_to_all x1, waiting for transfers between devices, body(): lax.all_to_all(author_out, 'paper', split_axis=0, concat_axis=0, tiled=True)  96.1 us
    all_to_all x1, waiting for transfers between devices, body(): lax.all_to_all(author_send, 'paper', split_axis=0, concat_axis=0, tiled=T...  80.4 us
    all_to_all x1, waiting for transfers between devices, body(): lax.all_to_all(outgoing_grad, 'paper', split_axis=0, concat_axis=0, tiled...  75.5 us
    all_to_all x1, blocking collectives, body(): lax.all_to_all(wanted_authors.reshape(peer_count, wslot_count), 'paper',...  22.3 us
    all_to_all x1, starting transfers between devices, body(): lax.all_to_all(outgoing_grad, 'paper', split_axis=0, concat_axis=0, tiled...  18.8 us
    all_gather x1, blocking collectives, body(): feats = lax.all_gather(paper_feat, 'author', axis=1, tiled=True)  11.6 us
    all_gather x1, blocking collectives, body(): writes = lax.all_gather(authorship_sum, 'author', axis=1, tiled=True)  11.5 us
    all_gather x1, blocking collectives, body(): cites = lax.all_gather(cite_sum, 'author', axis=1, tiled=True)  10.1 us
  transfers between devices with their start and end apart: 5, of which 3 were waited for; matrix products, arithmetic and copies ran while one was open for 23% of the time, Pallas kernels for 0%

commit v1 on v0

v1 whole, which is shorter than its diff:
```python
import functools

import jax
import jax.numpy as jnp
from jax import lax
from jax.experimental import pallas as pl
from jax.experimental.pallas import tpu as pltpu
from jax.sharding import PartitionSpec as P

MESH = pl.DeviceIdType.MESH
F32 = jnp.float32
BF16 = jnp.bfloat16
CORES = 2


def dot(left, right):
    return jnp.dot(left, right, preferred_element_type=F32)


def dot_left_flipped(left, right):
    return lax.dot_general(left, right, (((0,), (0,)), ((), ())), preferred_element_type=F32)


def dot_right_flipped(left, right):
    return lax.dot_general(left, right, (((1,), (1,)), ((), ())), preferred_element_type=F32)


def kernel(
    nx,
    nyc,
    nz,
    slot_tile,
    paper,
    author,
    cot,
    meta_f,
    meta_i,
    cite_tiles,
    write_tiles,
    w_self,
    w_cite,
    w_write,
    paper_out,
    paper_grad,
    author_grad,
    win,
    rows,
    feats,
    proj,
    slots,
    tiles,
    meta_fv,
    meta_iv,
    meta_fs,
    meta_is,
    acc,
    part_send,
    part_recv,
    pre,
    grads,
    grads_x,
    back_send,
    back_recv,
    sums,
    local_sem,
    feats_sem,
    meta_sem,
    tile_sem,
    share_sem,
    proj_sem,
    part_sem,
    grads_sem,
    grads_x_sem,
    back_sem,
    sums_sem,
):
    p = lax.axis_index("paper")
    x = lax.axis_index("author")
    z = p // nyc
    yc = p % nyc
    block = cite_tiles.shape[1]
    quarter = paper.shape[1]
    sent = []

    def send(src, dst, sems, index, device):
        copy = pltpu.make_async_remote_copy(
            src_ref=src,
            dst_ref=dst,
            send_sem=sems.at[(0,) + index],
            recv_sem=sems.at[(1,) + index],
            device_id=device,
            device_id_type=MESH,
        )
        copy.start()
        sent.append(copy)
        return copy

    def at_x(k):
        return (p, lax.rem(x + k + nx, nx))

    def at_yc(k):
        return (z * nyc + lax.rem(yc + k + nyc, nyc), x)

    def at_z(k):
        return (lax.rem(z + k + nz, nz) * nyc + yc, x)

    columns = pl.ds(pl.multiple_of(x * quarter, quarter), quarter)
    loads = []
    for i, w in enumerate((w_cite, w_write, w_self)):
        loads.append(pltpu.make_async_copy(w.at[:, columns], win.at[i], local_sem.at[i]))
        loads.append(pltpu.make_async_copy(w.at[columns, :], rows.at[i], local_sem.at[3 + i]))
    for load in loads:
        load.start()

    barrier = pltpu.get_barrier_semaphore()
    peers = [at_x(k) for k in range(1, nx)] + [at_yc(k) for k in range(1, nyc)] + [at_z(k) for k in range(1, nz)]
    for device in peers:
        pl.semaphore_signal(barrier, inc=1, device_id=device, device_id_type=MESH)
    pl.semaphore_wait(barrier, len(peers))

    feats_in = {}
    for m, own in enumerate((paper, author)):
        for k in range(1, nx):
            feats_in[m, k] = send(own, feats.at[m, x], feats_sem, (m, k), at_x(k))

    meta_in = []
    for k in range(1, nyc):
        to = lax.rem(yc + k, nyc)
        meta_in.append(send(meta_f.at[to], meta_fv.at[yc], meta_sem, (0, k), at_yc(k)))
        meta_in.append(send(meta_i.at[to], meta_iv.at[yc], meta_sem, (1, k), at_yc(k)))
    meta_fv[yc] = meta_f[yc]
    meta_iv[yc] = meta_i[yc]

    tiles_in = {}
    for m, source in enumerate((cite_tiles, write_tiles)):

        def place(i, carry):
            for j in range(nz):
                slots[m, i, j // 2, j % 2] = source[slot_tile[m, i * nz + j]]
            return carry

        lax.fori_loop(0, nyc, place, 0)
        for k in range(1, nyc):
            to = lax.rem(yc + k, nyc)
            for half in range(2):
                q = lax.rem(x + half, nx)
                tiles_in[m, k, half] = send(
                    slots.at[m, to, q], tiles.at[m, yc, q], tile_sem, (m, half, k), at_yc(k)
                )

    for load in loads:
        load.wait()
    turns = ((nz // 2, nz - 1 - nz // 2), (nz - 1 - nz // 2, nz // 2))
    ring = {}

    def pass_on(m, way, k):
        sign = 1 if way == 0 else -1
        origin = lax.rem(z - sign * (k - 1) + nz, nz)
        ring[m, way, k] = send(
            proj.at[m, origin], proj.at[m, origin], proj_sem, (m, way, k), at_z(sign)
        )

    for m, own in enumerate((paper, author)):
        feats[m, x] = own[...]
        for k in range(1, nx):
            feats_in[m, k].wait_recv()
        total = dot(feats[m, 0], win[m, 0:quarter, :])
        for i in range(1, nx):
            total += dot(feats[m, i], win[m, i * quarter : (i + 1) * quarter, :])
        total = total.astype(BF16)
        proj[m, z, 0] = total[0:block]
        proj[m, z, 1] = total[block:]
        for way in range(2):
            pass_on(m, way, 1)
    total = dot(feats[0, 0], win[2, 0:quarter, :])
    for i in range(1, nx):
        total += dot(feats[0, i], win[2, i * quarter : (i + 1) * quarter, :])
    pre[...] = total

    shared_in = {}
    for m in range(2):
        for k in range(1, nyc):
            origin = lax.rem(yc - k + nyc, nyc)
            for half in range(2):
                tiles_in[m, k, half].wait_recv()
                q = lax.rem(x + half, nx)
                place_at = tiles.at[m, origin, q]
                shared_in[m, k, half] = send(
                    place_at, place_at, share_sem, (m, half, k), at_x(1 if half == 0 else -1)
                )
        for k in range(2, nz // 2 + 1):
            if k - 1 <= nz // 2 and m == 0:
                for n in range(2):
                    for way in range(2):
                        if k <= turns[n][way]:
                            ring[n, way, k - 1].wait_recv()
                            pass_on(n, way, k)
    for m in range(2):
        for i in range(nx):
            tiles[m, yc, i] = slots[m, yc, i]
    for copy in meta_in:
        copy.wait_recv()
    small = [
        pltpu.make_async_copy(meta_fv, meta_fs, local_sem.at[6]),
        pltpu.make_async_copy(meta_iv, meta_is, local_sem.at[7]),
    ]
    for copy in small:
        copy.start()
    for copy in small:
        copy.wait()
    for n in range(2):
        for way in range(2):
            ring[n, way, turns[n][way]].wait_recv()

    def share_of(target):
        acc[...] = jnp.zeros_like(acc)

        def step(i, carry):
            m = i // nz
            s = i % nz
            source = meta_is[target, 0, i]
            product = dot(
                tiles[m, target, s // 2, s % 2],
                proj[m, s, source],
            )
            acc[0:block, :] += meta_fs[target, 0, i] * product
            acc[block:, :] += meta_fs[target, 1, i] * product
            return carry

        lax.fori_loop(0, 2 * nz, step, 0)

    share_of(yc)
    pre[...] += acc[...]
    part_in = []
    for k in range(1, nyc):
        for m in range(2):
            for half in range(2):
                shared_in[m, nyc - k, half].wait_recv()
        share_of(lax.rem(yc + k, nyc))
        part_send[k] = acc[...].astype(BF16)
        part_in.append(send(part_send.at[k], part_recv.at[k], part_sem, (k,), at_yc(k)))
    for k in range(1, nyc):
        part_in[k - 1].wait_recv()
        pre[...] += part_recv[k].astype(F32)

    preact = pre[...]
    sigma = jax.nn.sigmoid(preact)
    paper_out[...] = (paper[...].astype(F32) + preact * sigma).astype(BF16)
    slope = sigma * (1.0 + preact * (1.0 - sigma))
    own = (cot[...].astype(F32) * slope).astype(BF16)
    grads[yc, 0] = own[0:block]
    grads[yc, 1] = own[block:]
    grads_x[x] = own
    grads_in = [send(grads.at[yc], grads.at[yc], grads_sem, (k,), at_yc(k)) for k in range(1, nyc)]
    grads_x_in = [send(grads_x.at[x], grads_x.at[x], grads_x_sem, (k,), at_x(k)) for k in range(1, nx)]

    def back_of(m, place_z):
        acc[...] = jnp.zeros_like(acc)

        def step(i, carry):
            column = m * nz + place_z
            target = meta_is[i, 1, column]
            product = dot_left_flipped(
                tiles[m, i, place_z // 2, place_z % 2],
                grads[i, target],
            )
            acc[0:block, :] += meta_fs[i, 2, column] * product
            acc[block:, :] += meta_fs[i, 3, column] * product
            return carry

        lax.fori_loop(0, nyc, step, 0)

    for copy in grads_in:
        copy.wait_recv()
    back = {}
    for k in range(1, nz // 2 + 1):
        for m in range(2):
            for way in range(2):
                if k <= turns[m][way]:
                    sign = 1 if way == 0 else -1
                    distance = turns[m][way] - k + 1
                    back_of(m, lax.rem(z + sign * distance + nz, nz))
                    total = acc[...]
                    if k > 1:
                        back[m, way, k - 1].wait_recv()
                        total += back_recv[m, way, k - 1].astype(F32)
                    back_send[m, way, k] = total.astype(BF16)
                    back[m, way, k] = send(
                        back_send.at[m, way, k],
                        back_recv.at[m, way, k],
                        back_sem,
                        (m, way, k),
                        at_z(sign),
                    )

    for copy in grads_x_in:
        copy.wait_recv()
    total = cot[...].astype(F32)
    for i in range(nx):
        total += dot_right_flipped(grads_x[i], rows[2, :, i * quarter : (i + 1) * quarter])
    pre[...] = total
    sums_in = {}
    for m in range(2):
        back_of(m, z)
        total = acc[...]
        for way in range(2):
            back[m, way, turns[m][way]].wait_recv()
            total += back_recv[m, way, turns[m][way]].astype(F32)
        sums[m, x] = total.astype(BF16)
        for k in range(1, nx):
            sums_in[m, k] = send(sums.at[m, x], sums.at[m, x], sums_sem, (m, k), at_x(k))
    for m, out in enumerate((paper_grad, author_grad)):
        for k in range(1, nx):
            sums_in[m, k].wait_recv()
        total = dot_right_flipped(sums[m, 0], rows[m, :, 0:quarter])
        for i in range(1, nx):
            total += dot_right_flipped(sums[m, i], rows[m, :, i * quarter : (i + 1) * quarter])
        if m == 0:
            total += pre[...]
        out[...] = total.astype(BF16)
    for copy in sent:
        copy.wait_send()


def listing(owner, values, nyc, nz):
    places = jnp.arange(nz, dtype=jnp.int32)[None, :] * nyc + jnp.arange(nyc, dtype=jnp.int32)[:, None]
    named = owner[:, 0][:, None, None] == places[None]
    return jnp.sum(jnp.where(named[None], values[:, :, None, None], 0), axis=1)


def body(
    nx,
    paper_feat,
    author_feat,
    cite_owner,
    cite_source,
    cite_target,
    cite_edges,
    cite_count,
    citation_weight_tiles,
    write_owner,
    write_paper,
    write_author,
    write_edges,
    authorship_weight_tiles,
    w_self,
    w_cite,
    w_write,
    cotangent,
):
    nyc = 4 * CORES
    nz = lax.axis_size("paper") // nyc
    n_rows, quarter = paper_feat.shape
    block = citation_weight_tiles.shape[1]
    width = w_self.shape[0]

    live = jnp.arange(cite_edges.shape[0], dtype=jnp.int32) < cite_count[0]
    cite_scale = jnp.where(live, 1.0 / cite_edges.astype(F32), 0.0)
    write_scale = 1.0 / write_edges.astype(F32)
    floats, ints, order = [], [], []
    for owner, scale, target, source in (
        (cite_owner, cite_scale, cite_target, cite_source),
        (write_owner, write_scale, write_paper, write_author),
    ):
        floats.append(
            listing(
                owner,
                jnp.stack([
                    jnp.where(target == 0, scale, 0.0),
                    jnp.where(target == 1, scale, 0.0),
                    jnp.where(source == 0, scale, 0.0),
                    jnp.where(source == 1, scale, 0.0),
                ]),
                nyc,
                nz,
            )
        )
        number = jnp.arange(owner.shape[0], dtype=jnp.int32)
        found = listing(owner, jnp.stack([source, target, number]), nyc, nz)
        ints.append(found[:2])
        order.append(found[2].reshape(-1))

    def spread(parts):
        joined = jnp.stack(parts, axis=2)
        joined = joined.transpose(1, 0, 2, 3).reshape(nyc, -1, 2 * nz)
        return jnp.pad(joined, ((0, 0), (0, 8 - joined.shape[1]), (0, 128 - 2 * nz)))

    meta_f, meta_i, slot_tile = spread(floats), spread(ints), jnp.stack(order)
    steps = nz // 2 + 1
    vmem = pl.BlockSpec(memory_space=pltpu.VMEM)
    hbm = pl.BlockSpec(memory_space=pl.ANY)
    unit = jax.ShapeDtypeStruct((n_rows, quarter), BF16)

    def sems(*shape):
        return pltpu.SemaphoreType.DMA((2,) + shape)

    return pl.pallas_call(
        functools.partial(kernel, nx, nyc, nz),
        out_shape=(unit, unit, unit),
        in_specs=[pl.BlockSpec(memory_space=pltpu.SMEM)] + [vmem] * 7 + [hbm] * 3,
        out_specs=(vmem, vmem, vmem),
        scratch_shapes=[
            pltpu.VMEM((3, width, quarter), BF16),
            pltpu.VMEM((3, quarter, width), BF16),
            pltpu.VMEM((2, nx, n_rows, quarter), BF16),
            pltpu.VMEM((2, nz, 2, block, quarter), BF16),
            pltpu.VMEM((2, nyc, nz // 2, 2, block, block), BF16),
            pltpu.VMEM((2, nyc, nz // 2, 2, block, block), BF16),
            pltpu.VMEM((nyc, 8, 128), F32),
            pltpu.VMEM((nyc, 8, 128), jnp.int32),
            pltpu.SMEM((nyc, 8, 128), F32),
            pltpu.SMEM((nyc, 8, 128), jnp.int32),
            pltpu.VMEM((n_rows, quarter), F32),
            pltpu.VMEM((nyc, n_rows, quarter), BF16),
            pltpu.VMEM((nyc, n_rows, quarter), BF16),
            pltpu.VMEM((n_rows, quarter), F32),
            pltpu.VMEM((nyc, 2, block, quarter), BF16),
            pltpu.VMEM((nx, n_rows, quarter), BF16),
            pltpu.VMEM((2, 2, steps, n_rows, quarter), BF16),
            pltpu.VMEM((2, 2, steps, n_rows, quarter), BF16),
            pltpu.VMEM((2, nx, n_rows, quarter), BF16),
            pltpu.SemaphoreType.DMA((8,)),
            sems(2, nx),
            sems(2, nyc),
            sems(2, 2, nyc),
            sems(2, 2, nyc),
            sems(2, 2, steps),
            sems(nyc),
            sems(nyc),
            sems(nx),
            sems(2, 2, steps),
            sems(2, nx),
        ],
        compiler_params=pltpu.CompilerParams(
            collective_id=0, has_side_effects=True, vmem_limit_bytes=56 * 1024 * 1024
        ),
    )(
        slot_tile,
        paper_feat,
        author_feat,
        cotangent,
        meta_f,
        meta_i,
        citation_weight_tiles,
        authorship_weight_tiles,
        w_self,
        w_cite,
        w_write,
    )


def solution(mesh):
    in_specs = (
        P("paper", "author"),
        P("paper", "author"),
        P("paper", None),
        P("paper"),
        P("paper"),
        P("paper"),
        P("paper"),
        P("paper", None, None),
        P("paper", None),
        P("paper"),
        P("paper"),
        P("paper"),
        P("paper", None, None),
        P(),
        P(),
        P(),
        P("paper", "author"),
    )
    out_specs = (P("paper", "author"), P("paper", "author"), P("paper", "author"))
    return jax.shard_map(
        functools.partial(body, mesh.shape["author"]),
        mesh=mesh,
        in_specs=in_specs,
        out_specs=out_specs,
        check_vma=False,
    )
```

time: 499 us -> 150 us (0.30); the launches traced: 490 us -> 150 us
  waiting for transfers between devices: 253 us -> 0 us
  Pallas kernels: 0 us -> 135 us
  blocking collectives: 65.4 us -> 0 us
  matrix products: 54.6 us -> 0 us
  local copies, waits for them, and re-layouts: 51.6 us -> 6.34 us
  starting transfers between devices: 38.9 us -> 0 us
  between operations: 15.5 us -> 1.4 us
    all_to_all x4 -> x0, waiting for transfers between devices: 252 us -> none  [the longest x1 96.1 us: body(): lax.all_to_all(author_out, 'paper', split_axis=0, concat_axis=0, tiled=True)]
    pallas_call x0 -> x1, Pallas kernels: none -> 135 us  [body(): pl.pallas_call(functools.partial(kernel, nx, nyc, nz), out_shape=(unit, u...]
    dot_general x18 -> x0, matrix products: 54.6 us -> none  [the longest x1 8.6 us: body(): jnp.einsum('nr,nmh->rmh', slotted_target_index, partial_block_value, prec...]
    all_gather x4 -> x0, blocking collectives: 43.1 us -> none  [the longest x1 11.6 us: body(): feats = lax.all_gather(paper_feat, 'author', axis=1, tiled=True)]
    all_to_all x4 -> x0, starting transfers between devices: 38.8 us -> none  [the longest x1 18.8 us: body(): lax.all_to_all(outgoing_grad, 'paper', split_axis=0, concat_axis=0, tiled...]
    all_to_all x1 -> x0, blocking collectives: 22.3 us -> none  [body(): lax.all_to_all(wanted_authors.reshape(peer_count, wslot_count), 'paper',...]
    gather x5 -> x0, local copies, waits for them, and re-layouts: 17.7 us -> none  [the longest x1 6.16 us: body(): selected_rows = jnp.take(stacked, shard_of * paper_blocks + wanted, axis=0)]
    reshape x3 -> x2, local copies, waits for them, and re-layouts: 15.3 us -> 0.18 us  [spread(): joined = joined.transpose(1, 0, 2, 3).reshape(nyc, -1, 2 * nz)]
  transfers between devices with their start and end apart: 5 -> 0, of which waited for: 3 -> 0; matrix products, arithmetic and copies ran while one was open for 23% -> 0% of each run, Pallas kernels for 0% -> 0%
where the time goes in v1:
time: 150 us
  Pallas kernels  135 us (90%)
  other arithmetic  7.34 us (5%)
  local copies, waits for them, and re-layouts  6.34 us (4%)
    pallas_call x1, Pallas kernels, body(): pl.pallas_call(functools.partial(kernel, nx, nyc, nz), out_shape=(unit, u...  135 us
    unnamed x3, local copies, waits for them, and re-layouts  4.7 us

profile of v1, /device:TPU:1, one launch (start us, length us, event | category | flops | bytes accessed | tf_op | source)
XLA Modules:
  0.0 149.8 jit_solution(8108597825483560731)
XLA Ops:
  1.3 0.7 fusion
  2.0 0.7 fusion.4
  2.7 0.7 pad_add_fusion
  3.4 0.7 pad_add_fusion.1
  4.0 0.7 fusion.6
  4.7 0.7 fusion.2
  5.4 0.7 broadcast_compare_fusion
  6.2 0.7 broadcast_compare_fusion.1
  6.9 0.5 select_reduce_fusion.3
  7.4 0.1 stack_reshape_squeeze.6
  7.5 0.1 select_reduce_fusion.1
  7.6 0.5 select_reduce_fusion.2
  8.1 0.1 stack_reshape_squeeze.7
  8.2 0.6 pad_add_fusion.2.slot_tile
  8.8 0.1 reshape.46
  8.9 0.1 select_reduce_fusion
  9.0 0.1 reshape.45
  9.1 0.6 pad.8.meta_f
  9.7 0.6 pad.9.meta_i
  10.4 134.7 %shard_map.184 = (bf16[256,256]{1,0:T(8,128)(2,1)}, bf16[256,256]{1,0:T(8,128)(2,1)}, bf16[256,256]{1,0:T(8,128)(2,1)}) custom-call(s32[2,64]{1,0:T(2,128)} %pad_add_fusion.2.slot_tile, bf16[256,256]{1,0:T(8,128)(2,1)} %paper.1, bf16[256,256]{1,0:T(8,128)(2,1)} %author.1, bf16[256,256]{1,0:T(8,128)(2,1)} %cot.1, f32[8,8,128]{2,1,0:T(8,128)} %pad.8.meta_f, ...), custom_call_target="tpu_custom_call" | custom-call | tf_op jit(solution)/shard_map/pallas_call | solution.py:397
  145.1 1.6 %copy.27 = bf16[256,256]{1,0:T(8,128)(2,1)} copy(bf16[256,256]{1,0:T(8,128)(2,1)} %get-tuple-element.18) | data formatting | bytes 262144
  146.6 1.6 %copy.28 = bf16[256,256]{1,0:T(8,128)(2,1)} copy(bf16[256,256]{1,0:T(8,128)(2,1)} %get-tuple-element.19) | data formatting | bytes 262144
  148.2 1.6 %copy.29 = bf16[256,256]{1,0:T(8,128)(2,1)} copy(bf16[256,256]{1,0:T(8,128)(2,1)} %get-tuple-element.20) | data formatting | bytes 262144
  (13 shorter events, 0.1 us)

commit v2 on v1

v2 whole, which is shorter than its diff:
```python
import functools

import jax
import jax.numpy as jnp
from jax import lax
from jax.experimental import pallas as pl
from jax.experimental.pallas import tpu as pltpu
from jax.sharding import PartitionSpec as P

MESH = pl.DeviceIdType.MESH
F32 = jnp.float32
BF16 = jnp.bfloat16
CORES = 2


def dot(left, right):
    return jnp.dot(left, right, preferred_element_type=F32)


def dot_left_flipped(left, right):
    return lax.dot_general(left, right, (((0,), (0,)), ((), ())), preferred_element_type=F32)


def dot_right_flipped(left, right):
    return lax.dot_general(left, right, (((1,), (1,)), ((), ())), preferred_element_type=F32)


def kernel(
    nx,
    nyc,
    nz,
    cite_count,
    cite_owner,
    cite_source,
    cite_target,
    cite_edges,
    write_owner,
    write_author,
    write_paper,
    write_edges,
    paper,
    author,
    cot,
    cite_tiles_hbm,
    write_tiles_hbm,
    w_self,
    w_cite,
    w_write,
    paper_out,
    paper_grad,
    author_grad,
    cite_tiles,
    write_tiles,
    win,
    rows,
    feats,
    proj,
    meta_f,
    meta_i,
    slot_tab,
    slots,
    tiles,
    meta_fv,
    meta_iv,
    meta_fs,
    meta_is,
    acc,
    part_send,
    part_recv,
    pre,
    grads,
    grads_x,
    back_send,
    back_recv,
    sums,
    local_sem,
    feats_sem,
    meta_sem,
    tile_sem,
    share_sem,
    proj_sem,
    part_sem,
    grads_sem,
    grads_x_sem,
    back_sem,
    sums_sem,
):
    p = lax.axis_index("paper")
    x = lax.axis_index("author")
    z = p // nyc
    yc = p % nyc
    block = cite_tiles.shape[1]
    quarter = paper.shape[1]
    sent = []

    def send(src, dst, sems, index, device):
        copy = pltpu.make_async_remote_copy(
            src_ref=src,
            dst_ref=dst,
            send_sem=sems.at[(0,) + index],
            recv_sem=sems.at[(1,) + index],
            device_id=device,
            device_id_type=MESH,
        )
        copy.start()
        sent.append(copy)
        return copy

    def at_x(k):
        return (p, lax.rem(x + k + nx, nx))

    ny = nyc // CORES
    offsets = [(0, 1), (1, 0), (ny - 1, 0), (1, 1), (ny - 1, 1), (2, 0), (2, 1)]
    n_off = len(offsets)

    def there(k):
        dy, dc = offsets[k]
        return lax.rem(yc // CORES + dy, ny) * CORES + lax.rem(yc + dc, CORES)

    def back_from(k):
        dy, dc = offsets[k]
        return lax.rem(yc // CORES + ny - dy, ny) * CORES + lax.rem(yc + dc, CORES)

    def at_yc(k):
        return (z * nyc + there(k), x)

    def at_z(k):
        return (lax.rem(z + k + nz, nz) * nyc + yc, x)

    barrier = pltpu.get_barrier_semaphore()
    peers = [at_x(k) for k in range(1, nx)] + [at_yc(k) for k in range(n_off)] + [at_z(k) for k in range(1, nz)]
    for device in peers:
        pl.semaphore_signal(barrier, inc=1, device_id=device, device_id_type=MESH)

    tile_loads = [
        pltpu.make_async_copy(cite_tiles_hbm, cite_tiles, local_sem.at[6]),
        pltpu.make_async_copy(write_tiles_hbm, write_tiles, local_sem.at[7]),
    ]
    columns = pl.ds(pl.multiple_of(x * quarter, quarter), quarter)
    loads = []
    for i, w in enumerate((w_cite, w_write, w_self)):
        loads.append(pltpu.make_async_copy(w.at[:, columns], win.at[i], local_sem.at[i]))
        loads.append(pltpu.make_async_copy(w.at[columns, :], rows.at[i], local_sem.at[3 + i]))
    for load in tile_loads + loads:
        load.start()

    n_slots = nyc * nz
    lanes = lax.broadcasted_iota(jnp.int32, (n_slots, 128), 1)
    table_f = jnp.zeros((n_slots, 128), F32)
    table_i = jnp.zeros((n_slots, 128), jnp.int32)
    lists = (
        (cite_owner, cite_source, cite_target, cite_edges),
        (write_owner, write_author, write_paper, write_edges),
    )
    for m, (owner, sources, targets, edges) in enumerate(lists):
        n = owner.shape[1]
        number = lax.broadcasted_iota(jnp.int32, (n_slots, n), 1)
        slot = lax.broadcasted_iota(jnp.int32, (n_slots, n), 0)
        named = owner[...] == (slot % nz) * nyc + slot // nz
        scale = 1.0 / edges[...].astype(F32)
        source = jnp.max(jnp.where(named, sources[...], 0), axis=1, keepdims=True)
        target = jnp.max(jnp.where(named, targets[...], 0), axis=1, keepdims=True)
        place = jnp.max(jnp.where(named, number, 0), axis=1, keepdims=True)
        live = named & (number < cite_count[0]) if m == 0 else named
        scale = jnp.sum(jnp.where(live, scale, 0.0), axis=1, keepdims=True)
        for kind, value in enumerate((source, target, place)):
            table_i = jnp.where(lanes == 4 * m + kind, value, table_i)
        for kind, (end, b) in enumerate(((target, 0), (target, 1), (source, 0), (source, 1))):
            table_f = jnp.where(lanes == 4 * m + kind, jnp.where(end == b, scale, 0.0), table_f)
    meta_f[...] = table_f.reshape(nyc, nz, 128)
    meta_i[...] = table_i.reshape(nyc, nz, 128)
    tab = pltpu.make_async_copy(meta_i, slot_tab, local_sem.at[8])
    tab.start()
    meta_fv[yc] = meta_f[yc]
    meta_iv[yc] = meta_i[yc]

    pl.semaphore_wait(barrier, len(peers))

    feats_in = {}
    for m, own in enumerate((paper, author)):
        for k in range(1, nx):
            feats_in[m, k] = send(own, feats.at[m, x], feats_sem, (m, k), at_x(k))
    meta_in = []
    for k in range(n_off):
        to = there(k)
        meta_in.append(send(meta_f.at[to], meta_fv.at[yc], meta_sem, (0, k), at_yc(k)))
        meta_in.append(send(meta_i.at[to], meta_iv.at[yc], meta_sem, (1, k), at_yc(k)))

    tab.wait()
    for load in tile_loads:
        load.wait()
    tiles_in = {}
    for k in range(n_off):
        to = there(k)
        for m, source in enumerate((cite_tiles, write_tiles)):
            for j in range(nz):
                slots[m, to, j // 2, j % 2] = source[slot_tab[to, j, 4 * m + 2]]
            for half in range(nx if k == 0 else 2):
                q = lax.rem(x + half, nx)
                tiles_in[m, k, half] = send(
                    slots.at[m, to, q], tiles.at[m, yc, q], tile_sem, (m, half, k), at_yc(k)
                )
    for m, source in enumerate((cite_tiles, write_tiles)):
        for j in range(nz):
            tiles[m, yc, j // 2, j % 2] = source[slot_tab[yc, j, 4 * m + 2]]

    shared_in = {}

    def share_on(k):
        for m in range(2):
            for half in range(2):
                tiles_in[m, k, half].wait_recv()
                place_at = tiles.at[m, back_from(k), lax.rem(x + half, nx)]
                shared_in[m, k, half] = send(
                    place_at, place_at, share_sem, (m, half, k), at_x(1 if half == 0 else -1)
                )

    turns = ((nz // 2, nz - 1 - nz // 2), (nz - 1 - nz // 2, nz // 2))
    ring = {}

    def pass_on(m, way, k):
        sign = 1 if way == 0 else -1
        origin = lax.rem(z - sign * (k - 1) + nz, nz)
        ring[m, way, k] = send(
            proj.at[m, origin], proj.at[m, origin], proj_sem, (m, way, k), at_z(sign)
        )

    def ring_step(k):
        for m in range(2):
            for way in range(2):
                if k <= turns[m][way]:
                    ring[m, way, k - 1].wait_recv()
                    pass_on(m, way, k)

    def project(m, window):
        total = dot(feats[m, 0], win[window, 0:quarter, :])
        for i in range(1, nx):
            total += dot(feats[m, i], win[window, i * quarter : (i + 1) * quarter, :])
        return total

    for load in loads:
        load.wait()
    for m, own in enumerate((paper, author)):
        feats[m, x] = own[...]
        for k in range(1, nx):
            feats_in[m, k].wait_recv()
        total = project(m, m).astype(BF16)
        proj[m, z, 0] = total[0:block]
        proj[m, z, 1] = total[block:]
        for way in range(2):
            pass_on(m, way, 1)
        share_on(2 * m + 1)
        share_on(2 * m + 2)
    ring_step(2)
    pre[...] = project(0, 2)
    ring_step(3)
    share_on(5)
    share_on(6)
    ring_step(4)
    for copy in meta_in:
        copy.wait_recv()
    small = [
        pltpu.make_async_copy(meta_fv, meta_fs, local_sem.at[6]),
        pltpu.make_async_copy(meta_iv, meta_is, local_sem.at[7]),
    ]
    for copy in small:
        copy.start()
    for copy in small:
        copy.wait()
    for m in range(2):
        for way in range(2):
            ring[m, way, turns[m][way]].wait_recv()

    def share_of(target):
        acc[...] = jnp.zeros_like(acc)

        def step(i, carry):
            m = i // nz
            s = i % nz
            source = meta_is[target, s, 4 * m]
            product = dot(
                tiles[m, target, s // 2, s % 2],
                proj[m, s, source],
            )
            acc[0:block, :] += meta_fs[target, s, 4 * m] * product
            acc[block:, :] += meta_fs[target, s, 4 * m + 1] * product
            return carry

        lax.fori_loop(0, 2 * nz, step, 0)

    share_of(yc)
    pre[...] += acc[...]
    part_in = {}
    for k in range(n_off):
        opposite = (0, 2, 1, 4, 3, 5, 6)[k]
        if k == 0:
            for m in range(2):
                for half in range(nx):
                    tiles_in[m, k, half].wait_recv()
        else:
            for m in range(2):
                for half in range(2):
                    shared_in[m, k, half].wait_recv()
        share_of(there(opposite))
        part_send[opposite] = acc[...].astype(BF16)
        part_in[opposite] = send(
            part_send.at[opposite], part_recv.at[opposite], part_sem, (opposite,), at_yc(opposite)
        )
    for k in range(n_off):
        part_in[k].wait_recv()
        pre[...] += part_recv[k].astype(F32)

    preact = pre[...]
    sigma = jax.nn.sigmoid(preact)
    paper_out[...] = (paper[...].astype(F32) + preact * sigma).astype(BF16)
    slope = sigma * (1.0 + preact * (1.0 - sigma))
    own = (cot[...].astype(F32) * slope).astype(BF16)
    grads[yc, 0] = own[0:block]
    grads[yc, 1] = own[block:]
    grads_x[x] = own
    grads_in = [send(grads.at[yc], grads.at[yc], grads_sem, (k,), at_yc(k)) for k in range(n_off)]
    grads_x_in = [send(grads_x.at[x], grads_x.at[x], grads_x_sem, (k,), at_x(k)) for k in range(1, nx)]

    def back_of(m, place_z):
        acc[...] = jnp.zeros_like(acc)

        def step(i, carry):
            target = meta_is[i, place_z, 4 * m + 1]
            product = dot_left_flipped(
                tiles[m, i, place_z // 2, place_z % 2],
                grads[i, target],
            )
            acc[0:block, :] += meta_fs[i, place_z, 4 * m + 2] * product
            acc[block:, :] += meta_fs[i, place_z, 4 * m + 3] * product
            return carry

        lax.fori_loop(0, nyc, step, 0)

    for copy in grads_in:
        copy.wait_recv()
    back = {}
    for k in range(1, nz // 2 + 1):
        for m in range(2):
            for way in range(2):
                if k <= turns[m][way]:
                    sign = 1 if way == 0 else -1
                    distance = turns[m][way] - k + 1
                    back_of(m, lax.rem(z + sign * distance + nz, nz))
                    total = acc[...]
                    if k > 1:
                        back[m, way, k - 1].wait_recv()
                        total += back_recv[m, way, k - 1].astype(F32)
                    back_send[m, way, k] = total.astype(BF16)
                    back[m, way, k] = send(
                        back_send.at[m, way, k],
                        back_recv.at[m, way, k],
                        back_sem,
                        (m, way, k),
                        at_z(sign),
                    )

    for copy in grads_x_in:
        copy.wait_recv()
    total = cot[...].astype(F32)
    for i in range(nx):
        total += dot_right_flipped(grads_x[i], rows[2, :, i * quarter : (i + 1) * quarter])
    pre[...] = total
    sums_in = {}
    for m in range(2):
        back_of(m, z)
        total = acc[...]
        for way in range(2):
            back[m, way, turns[m][way]].wait_recv()
            total += back_recv[m, way, turns[m][way]].astype(F32)
        sums[m, x] = total.astype(BF16)
        for k in range(1, nx):
            sums_in[m, k] = send(sums.at[m, x], sums.at[m, x], sums_sem, (m, k), at_x(k))
    for m, out in enumerate((paper_grad, author_grad)):
        for k in range(1, nx):
            sums_in[m, k].wait_recv()
        total = dot_right_flipped(sums[m, 0], rows[m, :, 0:quarter])
        for i in range(1, nx):
            total += dot_right_flipped(sums[m, i], rows[m, :, i * quarter : (i + 1) * quarter])
        if m == 0:
            total += pre[...]
        out[...] = total.astype(BF16)
    for copy in sent:
        copy.wait_send()


def body(
    nx,
    paper_feat,
    author_feat,
    cite_owner,
    cite_source,
    cite_target,
    cite_edges,
    cite_count,
    citation_weight_tiles,
    write_owner,
    write_paper,
    write_author,
    write_edges,
    authorship_weight_tiles,
    w_self,
    w_cite,
    w_write,
    cotangent,
):
    nyc = 4 * CORES
    nz = lax.axis_size("paper") // nyc
    n_rows, quarter = paper_feat.shape
    block = citation_weight_tiles.shape[1]
    width = w_self.shape[0]

    lists = (
        cite_owner, cite_source, cite_target, cite_edges, write_owner, write_author, write_paper, write_edges
    )
    steps = nz // 2 + 1
    vmem = pl.BlockSpec(memory_space=pltpu.VMEM)
    hbm = pl.BlockSpec(memory_space=pl.ANY)
    unit = jax.ShapeDtypeStruct((n_rows, quarter), BF16)

    def sems(*shape):
        return pltpu.SemaphoreType.DMA((2,) + shape)

    return pl.pallas_call(
        functools.partial(kernel, nx, nyc, nz),
        out_shape=(unit, unit, unit),
        in_specs=[pl.BlockSpec(memory_space=pltpu.SMEM)] + [vmem] * 11 + [hbm] * 5,
        out_specs=(vmem, vmem, vmem),
        scratch_shapes=[
            pltpu.VMEM(citation_weight_tiles.shape, BF16),
            pltpu.VMEM(authorship_weight_tiles.shape, BF16),
            pltpu.VMEM((3, width, quarter), BF16),
            pltpu.VMEM((3, quarter, width), BF16),
            pltpu.VMEM((2, nx, n_rows, quarter), BF16),
            pltpu.VMEM((2, nz, 2, block, quarter), BF16),
            pltpu.VMEM((nyc, nz, 128), F32),
            pltpu.VMEM((nyc, nz, 128), jnp.int32),
            pltpu.SMEM((nyc, nz, 128), jnp.int32),
            pltpu.VMEM((2, nyc, nz // 2, 2, block, block), BF16),
            pltpu.VMEM((2, nyc, nz // 2, 2, block, block), BF16),
            pltpu.VMEM((nyc, nz, 128), F32),
            pltpu.VMEM((nyc, nz, 128), jnp.int32),
            pltpu.SMEM((nyc, nz, 128), F32),
            pltpu.SMEM((nyc, nz, 128), jnp.int32),
            pltpu.VMEM((n_rows, quarter), F32),
            pltpu.VMEM((nyc, n_rows, quarter), BF16),
            pltpu.VMEM((nyc, n_rows, quarter), BF16),
            pltpu.VMEM((n_rows, quarter), F32),
            pltpu.VMEM((nyc, 2, block, quarter), BF16),
            pltpu.VMEM((nx, n_rows, quarter), BF16),
            pltpu.VMEM((2, 2, steps, n_rows, quarter), BF16),
            pltpu.VMEM((2, 2, steps, n_rows, quarter), BF16),
            pltpu.VMEM((2, nx, n_rows, quarter), BF16),
            pltpu.SemaphoreType.DMA((9,)),
            sems(2, nx),
            sems(2, nyc),
            sems(2, nx, nyc),
            sems(2, 2, nyc),
            sems(2, 2, steps),
            sems(nyc),
            sems(nyc),
            sems(nx),
            sems(2, 2, steps),
            sems(2, nx),
        ],
        compiler_params=pltpu.CompilerParams(
            collective_id=0, has_side_effects=True, vmem_limit_bytes=56 * 1024 * 1024
        ),
    )(
        cite_count,
        *[a.reshape(1, -1) for a in lists],
        paper_feat,
        author_feat,
        cotangent,
        citation_weight_tiles,
        authorship_weight_tiles,
        w_self,
        w_cite,
        w_write,
    )


def solution(mesh):
    in_specs = (
        P("paper", "author"),
        P("paper", "author"),
        P("paper", None),
        P("paper"),
        P("paper"),
        P("paper"),
        P("paper"),
        P("paper", None, None),
        P("paper", None),
        P("paper"),
        P("paper"),
        P("paper"),
        P("paper", None, None),
        P(),
        P(),
        P(),
        P("paper", "author"),
    )
    out_specs = (P("paper", "author"), P("paper", "author"), P("paper", "author"))
    return jax.shard_map(
        functools.partial(body, mesh.shape["author"]),
        mesh=mesh,
        in_specs=in_specs,
        out_specs=out_specs,
        check_vma=False,
    )
```

time: 150 us -> 138 us (0.920)
  the two profiles are of different devices: /device:TPU:1 before, /device:TPU:16 now
where the time goes in v2:
time: 138 us
  Pallas kernels  132 us (96%)
  local copies, waits for them, and re-layouts  4.7 us (3%)
    pallas_call x1, Pallas kernels, body(): pl.pallas_call(functools.partial(kernel, nx, nyc, nz), out_shape=(unit, u...  132 us
    unnamed x3, local copies, waits for them, and re-layouts  4.7 us

profile of v2, /device:TPU:16, one launch (start us, length us, event | category | flops | bytes accessed | tf_op | source)
XLA Modules:
  0.0 137.7 jit_solution(7743341308604904500)
XLA Ops:
  1.3 131.7 %shard_map.184 = (bf16[256,256]{1,0:T(8,128)(2,1)}, bf16[256,256]{1,0:T(8,128)(2,1)}, bf16[256,256]{1,0:T(8,128)(2,1)}) custom-call(s32[1]{0:T(128)S(6)} %copy.23.cite_count, s32[1,48]{1,0:T(1,128)} %bitcast.8, s32[1,48]{1,0:T(1,128)} %bitcast.9, s32[1,48]{1,0:T(1,128)} %bitcast.10, s32[1,48]{1,0:T(1,128)} %bitcast.11, s32[1,32]{1,0:T(1,128)} %bitcast.12, ...), custom_call_target="tpu_custom_call" | custom-call | tf_op jit(solution)/shard_map/pallas_call | solution.py:428
  133.0 1.6 %copy.24 = bf16[256,256]{1,0:T(8,128)(2,1)} copy(bf16[256,256]{1,0:T(8,128)(2,1)} %get-tuple-element.6) | data formatting | bytes 262144
  134.6 1.6 %copy.25 = bf16[256,256]{1,0:T(8,128)(2,1)} copy(bf16[256,256]{1,0:T(8,128)(2,1)} %get-tuple-element.7) | data formatting | bytes 262144
  136.1 1.6 %copy.26 = bf16[256,256]{1,0:T(8,128)(2,1)} copy(bf16[256,256]{1,0:T(8,128)(2,1)} %get-tuple-element.8) | data formatting | bytes 262144

commit v3 on v2

--- a/solution.py
+++ b/solution.py
@@ -11,6 +11,7 @@
 F32 = jnp.float32
 BF16 = jnp.bfloat16
 CORES = 2
+UNROLL = 8
 
 
 def dot(left, right):
@@ -110,7 +111,8 @@
         return (p, lax.rem(x + k + nx, nx))
 
     ny = nyc // CORES
-    offsets = [(0, 1), (1, 0), (ny - 1, 0), (1, 1), (ny - 1, 1), (2, 0), (2, 1)]
+    offsets = [(0, 1), (1, 1), (ny - 1, 1), (2, 1), (1, 0), (ny - 1, 0), (2, 0)]
+    opposite = (0, 2, 1, 3, 5, 4, 6)
     n_off = len(offsets)
 
     def there(k):
@@ -126,6 +128,15 @@
 
     def at_z(k):
         return (lax.rem(z + k + nz, nz) * nyc + yc, x)
+
+    def gather_x(buffer, sems, m, own):
+        return {(m, k): send(own, buffer.at[m, x], sems, (m, k % nx), at_x(k)) for k in (1, -1)}
+
+    def chain_x(copies, buffer, sems, m):
+        onward = 1 if m == 0 else -1
+        copies[m, onward].wait_recv()
+        piece = buffer.at[m, lax.rem(x - onward + nx, nx)]
+        copies[m, 2] = send(piece, piece, sems, (m, 2), at_x(onward))
 
     barrier = pltpu.get_barrier_semaphore()
     peers = [at_x(k) for k in range(1, nx)] + [at_yc(k) for k in range(n_off)] + [at_z(k) for k in range(1, nz)]
@@ -176,10 +187,8 @@
 
     pl.semaphore_wait(barrier, len(peers))
 
-    feats_in = {}
-    for m, own in enumerate((paper, author)):
-        for k in range(1, nx):
-            feats_in[m, k] = send(own, feats.at[m, x], feats_sem, (m, k), at_x(k))
+    feats_in = gather_x(feats, feats_sem, 0, paper)
+    feats_in.update(gather_x(feats, feats_sem, 1, author))
     meta_in = []
     for k in range(n_off):
         to = there(k)
@@ -242,7 +251,10 @@
         load.wait()
     for m, own in enumerate((paper, author)):
         feats[m, x] = own[...]
-        for k in range(1, nx):
+        if m == 0:
+            for i in range(2):
+                chain_x(feats_in, feats, feats_sem, i)
+        for k in (-1 if m == 0 else 1, 2):
             feats_in[m, k].wait_recv()
         total = project(m, m).astype(BF16)
         proj[m, z, 0] = total[0:block]
@@ -286,27 +298,31 @@
             acc[block:, :] += meta_fs[target, s, 4 * m + 1] * product
             return carry
 
-        lax.fori_loop(0, 2 * nz, step, 0)
-
+        lax.fori_loop(0, 2 * nz, step, 0, unroll=UNROLL)
+
+    part_in = {}
+
+    def share_from(k):
+        for m in range(2):
+            for half in range(nx if k == 0 else 2):
+                (tiles_in if k == 0 else shared_in)[m, k, half].wait_recv()
+        share_of(there(opposite[k]))
+
+    def pass_part(slot, device):
+        part_send[slot] = acc[...].astype(BF16)
+        part_in[slot] = send(part_send.at[slot], part_recv.at[slot], part_sem, (slot,), device)
+
+    for k in range(ny):
+        share_from(k)
+        pass_part(opposite[k], at_yc(0))
+    for k in range(ny, n_off):
+        share_from(k)
+        part_in[opposite[k] - ny + 1].wait_recv()
+        acc[...] += part_recv[opposite[k] - ny + 1].astype(F32)
+        pass_part(opposite[k], at_yc(opposite[k]))
     share_of(yc)
     pre[...] += acc[...]
-    part_in = {}
-    for k in range(n_off):
-        opposite = (0, 2, 1, 4, 3, 5, 6)[k]
-        if k == 0:
-            for m in range(2):
-                for half in range(nx):
-                    tiles_in[m, k, half].wait_recv()
-        else:
-            for m in range(2):
-                for half in range(2):
-                    shared_in[m, k, half].wait_recv()
-        share_of(there(opposite))
-        part_send[opposite] = acc[...].astype(BF16)
-        part_in[opposite] = send(
-            part_send.at[opposite], part_recv.at[opposite], part_sem, (opposite,), at_yc(opposite)
-        )
-    for k in range(n_off):
+    for k in (0,) + tuple(range(ny, n_off)):
         part_in[k].wait_recv()
         pre[...] += part_recv[k].astype(F32)
 
@@ -318,8 +334,13 @@
     grads[yc, 0] = own[0:block]
     grads[yc, 1] = own[block:]
     grads_x[x] = own
-    grads_in = [send(grads.at[yc], grads.at[yc], grads_sem, (k,), at_yc(k)) for k in range(n_off)]
+    grads_in = {k: send(grads.at[yc], grads.at[yc], grads_sem, (k,), at_yc(k)) for k in range(ny, n_off)}
+    grads_in[0] = send(grads.at[yc], grads.at[yc], grads_sem, (0,), at_yc(0))
     grads_x_in = [send(grads_x.at[x], grads_x.at[x], grads_x_sem, (k,), at_x(k)) for k in range(1, nx)]
+    for k in range(ny, n_off):
+        grads_in[k].wait_recv()
+        piece = grads.at[back_from(k)]
+        grads_in[k - ny + 1] = send(piece, piece, grads_sem, (k - ny + 1,), at_yc(0))
 
     def back_of(m, place_z):
         acc[...] = jnp.zeros_like(acc)
@@ -334,10 +355,10 @@
             acc[block:, :] += meta_fs[i, place_z, 4 * m + 3] * product
             return carry
 
-        lax.fori_loop(0, nyc, step, 0)
-
-    for copy in grads_in:
-        copy.wait_recv()
+        lax.fori_loop(0, nyc, step, 0, unroll=UNROLL)
+
+    for k in range(ny):
+        grads_in[k].wait_recv()
     back = {}
     for k in range(1, nz // 2 + 1):
         for m in range(2):
@@ -373,10 +394,11 @@
             back[m, way, turns[m][way]].wait_recv()
             total += back_recv[m, way, turns[m][way]].astype(F32)
         sums[m, x] = total.astype(BF16)
-        for k in range(1, nx):
-            sums_in[m, k] = send(sums.at[m, x], sums.at[m, x], sums_sem, (m, k), at_x(k))
+        sums_in.update(gather_x(sums, sums_sem, m, sums.at[m, x]))
+    for m in range(2):
+        chain_x(sums_in, sums, sums_sem, m)
     for m, out in enumerate((paper_grad, author_grad)):
-        for k in range(1, nx):
+        for k in (-1 if m == 0 else 1, 2):
             sums_in[m, k].wait_recv()
         total = dot_right_flipped(sums[m, 0], rows[m, :, 0:quarter])
         for i in range(1, nx):

time: 138 us -> 115 us (0.83)
  the two profiles are of different devices: /device:TPU:16 before, /device:TPU:1 now
where the time goes in v3:
time: 115 us; the launch traced here: 114 us
  Pallas kernels  108 us (94%)
  local copies, waits for them, and re-layouts  4.7 us (4%)
  between operations  1.29 us (1%)
    pallas_call x1, Pallas kernels, body(): pl.pallas_call(functools.partial(kernel, nx, nyc, nz), out_shape=(unit, u...  108 us
    unnamed x3, local copies, waits for them, and re-layouts  4.7 us

profile of v3, /device:TPU:1, one launch (start us, length us, event | category | flops | bytes accessed | tf_op | source)
XLA Modules:
  0.0 114.5 jit_solution(17954559856705288139)
XLA Ops:
  1.3 108.5 %shard_map.184 = (bf16[256,256]{1,0:T(8,128)(2,1)}, bf16[256,256]{1,0:T(8,128)(2,1)}, bf16[256,256]{1,0:T(8,128)(2,1)}) custom-call(s32[1]{0:T(128)S(6)} %copy.23.cite_count, s32[1,48]{1,0:T(1,128)} %bitcast.8, s32[1,48]{1,0:T(1,128)} %bitcast.9, s32[1,48]{1,0:T(1,128)} %bitcast.10, s32[1,48]{1,0:T(1,128)} %bitcast.11, s32[1,32]{1,0:T(1,128)} %bitcast.12, ...), custom_call_target="tpu_custom_call" | custom-call | tf_op jit(solution)/shard_map/pallas_call | solution.py:450
  109.8 1.6 %copy.24 = bf16[256,256]{1,0:T(8,128)(2,1)} copy(bf16[256,256]{1,0:T(8,128)(2,1)} %get-tuple-element.6) | data formatting | bytes 262144
  111.3 1.6 %copy.25 = bf16[256,256]{1,0:T(8,128)(2,1)} copy(bf16[256,256]{1,0:T(8,128)(2,1)} %get-tuple-element.7) | data formatting | bytes 262144
  112.9 1.6 %copy.26 = bf16[256,256]{1,0:T(8,128)(2,1)} copy(bf16[256,256]{1,0:T(8,128)(2,1)} %get-tuple-element.8) | data formatting | bytes 262144

commit v4 on v3

--- a/solution.py
+++ b/solution.py
@@ -130,16 +130,27 @@
         return (lax.rem(z + k + nz, nz) * nyc + yc, x)
 
     def gather_x(buffer, sems, m, own):
-        return {(m, k): send(own, buffer.at[m, x], sems, (m, k % nx), at_x(k)) for k in (1, -1)}
+        piece = buffer.at[m, x]
+        copies = {}
+        for k in (1, -1):
+            if own is None:
+                copies[k] = send(piece, piece, sems, (m, k % nx), at_x(k))
+            else:
+                copies[k] = send(own, piece, sems, (m, k % nx), at_x(k))
+        return copies
 
     def chain_x(copies, buffer, sems, m):
-        onward = 1 if m == 0 else -1
-        copies[m, onward].wait_recv()
-        piece = buffer.at[m, lax.rem(x - onward + nx, nx)]
-        copies[m, 2] = send(piece, piece, sems, (m, 2), at_x(onward))
+        for b, onward in ((0, 1), (1, -1)):
+            copies[onward].wait_recv()
+            piece = buffer.at[m, lax.rem(x - onward + nx, nx), pl.ds(b * block, block)]
+            copies[2 + b] = send(piece, piece, sems, (m, 2 * b), at_x(onward))
+
+    def end_x(copies):
+        for b in range(2):
+            copies[2 + b].wait_recv()
 
     barrier = pltpu.get_barrier_semaphore()
-    peers = [at_x(k) for k in range(1, nx)] + [at_yc(k) for k in range(n_off)] + [at_z(k) for k in range(1, nz)]
+    peers = [at_x(k) for k in range(1, nx)] + [at_yc(k) for k in range(n_off)] + [at_z(1), at_z(-1)]
     for device in peers:
         pl.semaphore_signal(barrier, inc=1, device_id=device, device_id_type=MESH)
 
@@ -187,8 +198,7 @@
 
     pl.semaphore_wait(barrier, len(peers))
 
-    feats_in = gather_x(feats, feats_sem, 0, paper)
-    feats_in.update(gather_x(feats, feats_sem, 1, author))
+    feats_x = gather_x(feats, feats_sem, 0, paper)
     meta_in = []
     for k in range(n_off):
         to = there(k)
@@ -199,7 +209,9 @@
     for load in tile_loads:
         load.wait()
     tiles_in = {}
-    for k in range(n_off):
+    shared_in = {}
+
+    def tiles_out(k):
         to = there(k)
         for m, source in enumerate((cite_tiles, write_tiles)):
             for j in range(nz):
@@ -209,11 +221,6 @@
                 tiles_in[m, k, half] = send(
                     slots.at[m, to, q], tiles.at[m, yc, q], tile_sem, (m, half, k), at_yc(k)
                 )
-    for m, source in enumerate((cite_tiles, write_tiles)):
-        for j in range(nz):
-            tiles[m, yc, j // 2, j % 2] = source[slot_tab[yc, j, 4 * m + 2]]
-
-    shared_in = {}
 
     def share_on(k):
         for m in range(2):
@@ -224,22 +231,22 @@
                     place_at, place_at, share_sem, (m, half, k), at_x(1 if half == 0 else -1)
                 )
 
-    turns = ((nz // 2, nz - 1 - nz // 2), (nz - 1 - nz // 2, nz // 2))
+    far = nz // 2
+    turns = ((far, nz - 1 - far), (nz - 1 - far, far))
     ring = {}
 
-    def pass_on(m, way, k):
+    def pass_on(m, b, way, k):
         sign = 1 if way == 0 else -1
-        origin = lax.rem(z - sign * (k - 1) + nz, nz)
-        ring[m, way, k] = send(
-            proj.at[m, origin], proj.at[m, origin], proj_sem, (m, way, k), at_z(sign)
-        )
-
-    def ring_step(k):
-        for m in range(2):
-            for way in range(2):
-                if k <= turns[m][way]:
-                    ring[m, way, k - 1].wait_recv()
-                    pass_on(m, way, k)
+        piece = proj.at[m, lax.rem(z - sign * (k - 1) + nz, nz), b]
+        ring[m, b, way, k] = send(piece, piece, proj_sem, (m, b, way, k), at_z(sign))
+
+    def ring_step(m, k):
+        for way in range(2):
+            for b in range(2):
+                if k <= turns[b][way]:
+                    if k > 1:
+                        ring[m, b, way, k - 1].wait_recv()
+                    pass_on(m, b, way, k)
 
     def project(m, window):
         total = dot(feats[m, 0], win[window, 0:quarter, :])
@@ -247,28 +254,45 @@
             total += dot(feats[m, i], win[window, i * quarter : (i + 1) * quarter, :])
         return total
 
-    for load in loads:
-        load.wait()
-    for m, own in enumerate((paper, author)):
-        feats[m, x] = own[...]
-        if m == 0:
-            for i in range(2):
-                chain_x(feats_in, feats, feats_sem, i)
-        for k in (-1 if m == 0 else 1, 2):
-            feats_in[m, k].wait_recv()
+    def project_own(m):
         total = project(m, m).astype(BF16)
         proj[m, z, 0] = total[0:block]
         proj[m, z, 1] = total[block:]
-        for way in range(2):
-            pass_on(m, way, 1)
-        share_on(2 * m + 1)
-        share_on(2 * m + 2)
-    ring_step(2)
+        ring_step(m, 1)
+
+    for k in range(3):
+        tiles_out(k)
+    chain_x(feats_x, feats, feats_sem, 0)
+    feats_y = gather_x(feats, feats_sem, 1, author)
+    tiles_out(3)
+    feats[0, x] = paper[...]
+    feats[1, x] = author[...]
+    for load in loads:
+        load.wait()
+    end_x(feats_x)
+    project_own(0)
+    share_on(1)
+    share_on(2)
+    tiles_out(4)
+    tiles_out(5)
+    chain_x(feats_y, feats, feats_sem, 1)
+    ring_step(0, 2)
+    end_x(feats_y)
+    project_own(1)
+    share_on(3)
+    tiles_out(6)
+    ring_step(0, 3)
     pre[...] = project(0, 2)
-    ring_step(3)
+    for m, source in enumerate((cite_tiles, write_tiles)):
+        for j in range(nz):
+            tiles[m, yc, j // 2, j % 2] = source[slot_tab[yc, j, 4 * m + 2]]
+    ring_step(1, 2)
+    share_on(4)
     share_on(5)
+    ring_step(0, 4)
+    ring_step(1, 3)
     share_on(6)
-    ring_step(4)
+    ring_step(1, 4)
     for copy in meta_in:
         copy.wait_recv()
     small = [
@@ -280,8 +304,9 @@
     for copy in small:
         copy.wait()
     for m in range(2):
-        for way in range(2):
-            ring[m, way, turns[m][way]].wait_recv()
+        for b in range(2):
+            for way in range(2):
+                ring[m, b, way, turns[b][way]].wait_recv()
 
     def share_of(target):
         acc[...] = jnp.zeros_like(acc)
@@ -360,25 +385,33 @@
     for k in range(ny):
         grads_in[k].wait_recv()
     back = {}
-    for k in range(1, nz // 2 + 1):
-        for m in range(2):
-            for way in range(2):
-                if k <= turns[m][way]:
-                    sign = 1 if way == 0 else -1
-                    distance = turns[m][way] - k + 1
-                    back_of(m, lax.rem(z + sign * distance + nz, nz))
-                    total = acc[...]
-                    if k > 1:
-                        back[m, way, k - 1].wait_recv()
-                        total += back_recv[m, way, k - 1].astype(F32)
-                    back_send[m, way, k] = total.astype(BF16)
-                    back[m, way, k] = send(
-                        back_send.at[m, way, k],
-                        back_recv.at[m, way, k],
-                        back_sem,
-                        (m, way, k),
-                        at_z(sign),
-                    )
+
+    def back_on(m, b, way, distance):
+        k = turns[b][way] - distance + 1
+        total = acc[b * block : (b + 1) * block, :]
+        if k > 1:
+            back[m, b, way, k - 1].wait_recv()
+            total += back_recv[m, b, way, k - 1].astype(F32)
+        back_send[m, b, way, k] = total.astype(BF16)
+        back[m, b, way, k] = send(
+            back_send.at[m, b, way, k],
+            back_recv.at[m, b, way, k],
+            back_sem,
+            (m, b, way, k),
+            at_z(1 if way == 0 else -1),
+        )
+
+    for distance in range(far, 0, -1):
+        for way in range(2):
+            for m in range(2):
+                if distance < far:
+                    back_of(m, lax.rem(z + (distance if way == 0 else nz - distance), nz))
+                    for b in (way, 1 - way):
+                        back_on(m, b, way, distance)
+                elif way == 0:
+                    back_of(m, lax.rem(z + far, nz))
+                    back_on(m, 0, 0, far)
+                    back_on(m, 1, 1, far)
 
     for copy in grads_x_in:
         copy.wait_recv()
@@ -389,17 +422,17 @@
     sums_in = {}
     for m in range(2):
         back_of(m, z)
-        total = acc[...]
-        for way in range(2):
-            back[m, way, turns[m][way]].wait_recv()
-            total += back_recv[m, way, turns[m][way]].astype(F32)
-        sums[m, x] = total.astype(BF16)
-        sums_in.update(gather_x(sums, sums_sem, m, sums.at[m, x]))
+        for b in range(2):
+            total = acc[b * block : (b + 1) * block, :]
+            for way in range(2):
+                back[m, b, way, turns[b][way]].wait_recv()
+                total += back_recv[m, b, way, turns[b][way]].astype(F32)
+            sums[m, x, pl.ds(b * block, block)] = total.astype(BF16)
+        sums_in[m] = gather_x(sums, sums_sem, m, None)
     for m in range(2):
-        chain_x(sums_in, sums, sums_sem, m)
+        chain_x(sums_in[m], sums, sums_sem, m)
     for m, out in enumerate((paper_grad, author_grad)):
-        for k in (-1 if m == 0 else 1, 2):
-            sums_in[m, k].wait_recv()
+        end_x(sums_in[m])
         total = dot_right_flipped(sums[m, 0], rows[m, :, 0:quarter])
         for i in range(1, nx):
             total += dot_right_flipped(sums[m, i], rows[m, :, i * quarter : (i + 1) * quarter])
@@ -447,7 +480,7 @@
     def sems(*shape):
         return pltpu.SemaphoreType.DMA((2,) + shape)
 
-    return pl.pallas_call(
+    results = pl.pallas_call(
         functools.partial(kernel, nx, nyc, nz),
         out_shape=(unit, unit, unit),
         in_specs=[pl.BlockSpec(memory_space=pltpu.SMEM)] + [vmem] * 11 + [hbm] * 5,
@@ -474,19 +507,19 @@
             pltpu.VMEM((n_rows, quarter), F32),
             pltpu.VMEM((nyc, 2, block, quarter), BF16),
             pltpu.VMEM((nx, n_rows, quarter), BF16),
-            pltpu.VMEM((2, 2, steps, n_rows, quarter), BF16),
-            pltpu.VMEM((2, 2, steps, n_rows, quarter), BF16),
+            pltpu.VMEM((2, 2, 2, steps, block, quarter), BF16),
+            pltpu.VMEM((2, 2, 2, steps, block, quarter), BF16),
             pltpu.VMEM((2, nx, n_rows, quarter), BF16),
             pltpu.SemaphoreType.DMA((9,)),
             sems(2, nx),
             sems(2, nyc),
             sems(2, nx, nyc),
             sems(2, 2, nyc),
-            sems(2, 2, steps),
+            sems(2, 2, 2, steps),
             sems(nyc),
             sems(nyc),
             sems(nx),
-            sems(2, 2, steps),
+            sems(2, 2, 2, steps),
             sems(2, nx),
         ],
         compiler_params=pltpu.CompilerParams(
@@ -504,6 +537,21 @@
         w_cite,
         w_write,
     )
+    return pl.pallas_call(
+        hand_over,
+        out_shape=(unit, unit, unit),
+        in_specs=[hbm] * 3,
+        out_specs=(hbm, hbm, hbm),
+        scratch_shapes=[pltpu.SemaphoreType.DMA((3,))],
+    )(*results)
+
+
+def hand_over(*refs):
+    copies = [pltpu.make_async_copy(refs[i], refs[3 + i], refs[6].at[i]) for i in range(3)]
+    for copy in copies:
+        copy.start()
+    for copy in copies:
+        copy.wait()
 
 
 def solution(mesh):

time: 115 us -> 122 us (1.061)
  Pallas kernels: 108 us -> 120 us
  local copies, waits for them, and re-layouts: 4.7 us -> 0 us
    pallas_call x0 -> x1, Pallas kernels: none -> 13 us  [body(): pl.pallas_call(hand_over, out_shape=(unit, unit, unit), in_specs=[hbm] *...]
    unnamed x3 -> x0, local copies, waits for them, and re-layouts: 4.7 us -> none
    pallas_call x1, Pallas kernels: 108 us -> 107 us  [body(): pl.pallas_call(functools.partial(kernel, nx, nyc, nz), out_shape=(unit, u...]
where the time goes in v4:
time: 122 us
  Pallas kernels  120 us (98%)
  between operations  1.45 us (1%)
    pallas_call x1, Pallas kernels, body(): pl.pallas_call(functools.partial(kernel, nx, nyc, nz), out_shape=(unit, u...  107 us
    pallas_call x1, Pallas kernels, body(): pl.pallas_call(hand_over, out_shape=(unit, unit, unit), in_specs=[hbm] *...  13 us

profile of v4, /device:TPU:1, one launch (start us, length us, event | category | flops | bytes accessed | tf_op | source)
XLA Modules:
  0.0 121.5 jit_solution(856327274718262106)
XLA Ops:
  1.3 107.0 %shard_map.184 = (bf16[256,256]{1,0:T(8,128)(2,1)}, bf16[256,256]{1,0:T(8,128)(2,1)}, bf16[256,256]{1,0:T(8,128)(2,1)}) custom-call(s32[1]{0:T(128)S(6)} %copy.20.cite_count, s32[1,48]{1,0:T(1,128)} %bitcast.8, s32[1,48]{1,0:T(1,128)} %bitcast.9, s32[1,48]{1,0:T(1,128)} %bitcast.10, s32[1,48]{1,0:T(1,128)} %bitcast.11, s32[1,32]{1,0:T(1,128)} %bitcast.12, ...), custom_call_target="tpu_custom_call" | custom-call | tf_op jit(solution)/shard_map/pallas_call | solution.py:483
  108.3 13.0 %shard_map.185 = (bf16[256,256]{1,0:T(8,128)(2,1)}, bf16[256,256]{1,0:T(8,128)(2,1)}, bf16[256,256]{1,0:T(8,128)(2,1)}) custom-call(bf16[256,256]{1,0:T(8,128)(2,1)} %get-tuple-element.6.refs_0_, bf16[256,256]{1,0:T(8,128)(2,1)} %get-tuple-element.7.refs_1_, bf16[256,256]{1,0:T(8,128)(2,1)} %get-tuple-element.8.refs_2_), custom_call_target="tpu_custom_call" | custom-call | tf_op jit(solution)/shard_map/pallas_call | solution.py:540

commit v5 on v4

--- a/solution.py
+++ b/solution.py
@@ -31,25 +31,29 @@
     nyc,
     nz,
     cite_count,
-    cite_owner,
-    cite_source,
-    cite_target,
-    cite_edges,
-    write_owner,
-    write_author,
-    write_paper,
-    write_edges,
-    paper,
-    author,
-    cot,
+    cite_owner_hbm,
+    cite_source_hbm,
+    cite_target_hbm,
+    cite_edges_hbm,
+    write_owner_hbm,
+    write_author_hbm,
+    write_paper_hbm,
+    write_edges_hbm,
+    paper_hbm,
+    author_hbm,
+    cot_hbm,
     cite_tiles_hbm,
     write_tiles_hbm,
     w_self,
     w_cite,
     w_write,
-    paper_out,
-    paper_grad,
-    author_grad,
+    paper_out_hbm,
+    paper_grad_hbm,
+    author_grad_hbm,
+    cite_lists,
+    write_lists,
+    cot,
+    outs,
     cite_tiles,
     write_tiles,
     win,
@@ -90,8 +94,8 @@
     x = lax.axis_index("author")
     z = p // nyc
     yc = p % nyc
-    block = cite_tiles.shape[1]
-    quarter = paper.shape[1]
+    block = cite_tiles_hbm.shape[1]
+    quarter = paper_hbm.shape[1]
     sent = []
 
     def send(src, dst, sems, index, device):
@@ -129,15 +133,9 @@
     def at_z(k):
         return (lax.rem(z + k + nz, nz) * nyc + yc, x)
 
-    def gather_x(buffer, sems, m, own):
+    def gather_x(buffer, sems, m):
         piece = buffer.at[m, x]
-        copies = {}
-        for k in (1, -1):
-            if own is None:
-                copies[k] = send(piece, piece, sems, (m, k % nx), at_x(k))
-            else:
-                copies[k] = send(own, piece, sems, (m, k % nx), at_x(k))
-        return copies
+        return {k: send(piece, piece, sems, (m, k % nx), at_x(k)) for k in (1, -1)}
 
     def chain_x(copies, buffer, sems, m):
         for b, onward in ((0, 1), (1, -1)):
@@ -154,6 +152,20 @@
     for device in peers:
         pl.semaphore_signal(barrier, inc=1, device_id=device, device_id_type=MESH)
 
+    paper, author = feats.at[0, x], feats.at[1, x]
+    own_loads = [
+        pltpu.make_async_copy(paper_hbm, paper, local_sem.at[9]),
+        pltpu.make_async_copy(author_hbm, author, local_sem.at[10]),
+        pltpu.make_async_copy(cot_hbm, cot, local_sem.at[11]),
+    ]
+    list_loads = [
+        pltpu.make_async_copy(source, into.at[i], local_sem.at[12 + 4 * m + i])
+        for m, into, sources in (
+            (0, cite_lists, (cite_owner_hbm, cite_source_hbm, cite_target_hbm, cite_edges_hbm)),
+            (1, write_lists, (write_owner_hbm, write_author_hbm, write_paper_hbm, write_edges_hbm)),
+        )
+        for i, source in enumerate(sources)
+    ]
     tile_loads = [
         pltpu.make_async_copy(cite_tiles_hbm, cite_tiles, local_sem.at[6]),
         pltpu.make_async_copy(write_tiles_hbm, write_tiles, local_sem.at[7]),
@@ -163,25 +175,24 @@
     for i, w in enumerate((w_cite, w_write, w_self)):
         loads.append(pltpu.make_async_copy(w.at[:, columns], win.at[i], local_sem.at[i]))
         loads.append(pltpu.make_async_copy(w.at[columns, :], rows.at[i], local_sem.at[3 + i]))
-    for load in tile_loads + loads:
+    for load in list_loads + own_loads + tile_loads + loads:
         load.start()
+    for load in list_loads:
+        load.wait()
 
     n_slots = nyc * nz
     lanes = lax.broadcasted_iota(jnp.int32, (n_slots, 128), 1)
     table_f = jnp.zeros((n_slots, 128), F32)
     table_i = jnp.zeros((n_slots, 128), jnp.int32)
-    lists = (
-        (cite_owner, cite_source, cite_target, cite_edges),
-        (write_owner, write_author, write_paper, write_edges),
-    )
-    for m, (owner, sources, targets, edges) in enumerate(lists):
-        n = owner.shape[1]
+    for m, lists in enumerate((cite_lists, write_lists)):
+        owner, sources, targets, edges = lists[0], lists[1], lists[2], lists[3]
+        n = lists.shape[2]
         number = lax.broadcasted_iota(jnp.int32, (n_slots, n), 1)
         slot = lax.broadcasted_iota(jnp.int32, (n_slots, n), 0)
-        named = owner[...] == (slot % nz) * nyc + slot // nz
-        scale = 1.0 / edges[...].astype(F32)
-        source = jnp.max(jnp.where(named, sources[...], 0), axis=1, keepdims=True)
-        target = jnp.max(jnp.where(named, targets[...], 0), axis=1, keepdims=True)
+        named = owner == (slot % nz) * nyc + slot // nz
+        scale = 1.0 / edges.astype(F32)
+        source = jnp.max(jnp.where(named, sources, 0), axis=1, keepdims=True)
+        target = jnp.max(jnp.where(named, targets, 0), axis=1, keepdims=True)
         place = jnp.max(jnp.where(named, number, 0), axis=1, keepdims=True)
         live = named & (number < cite_count[0]) if m == 0 else named
         scale = jnp.sum(jnp.where(live, scale, 0.0), axis=1, keepdims=True)
@@ -198,7 +209,10 @@
 
     pl.semaphore_wait(barrier, len(peers))
 
-    feats_x = gather_x(feats, feats_sem, 0, paper)
+    for load in own_loads:
+        load.wait()
+    feats_x = gather_x(feats, feats_sem, 0)
+    feats_y = gather_x(feats, feats_sem, 1)
     meta_in = []
     for k in range(n_off):
         to = there(k)
@@ -263,36 +277,33 @@
     for k in range(3):
         tiles_out(k)
     chain_x(feats_x, feats, feats_sem, 0)
-    feats_y = gather_x(feats, feats_sem, 1, author)
     tiles_out(3)
-    feats[0, x] = paper[...]
-    feats[1, x] = author[...]
+    chain_x(feats_y, feats, feats_sem, 1)
+    tiles_out(4)
     for load in loads:
         load.wait()
     end_x(feats_x)
     project_own(0)
+    tiles_out(5)
+    end_x(feats_y)
+    project_own(1)
+    tiles_out(6)
     share_on(1)
     share_on(2)
-    tiles_out(4)
-    tiles_out(5)
-    chain_x(feats_y, feats, feats_sem, 1)
     ring_step(0, 2)
-    end_x(feats_y)
-    project_own(1)
+    ring_step(1, 2)
     share_on(3)
-    tiles_out(6)
-    ring_step(0, 3)
     pre[...] = project(0, 2)
     for m, source in enumerate((cite_tiles, write_tiles)):
         for j in range(nz):
             tiles[m, yc, j // 2, j % 2] = source[slot_tab[yc, j, 4 * m + 2]]
-    ring_step(1, 2)
+    ring_step(0, 3)
+    ring_step(1, 3)
     share_on(4)
     share_on(5)
     ring_step(0, 4)
-    ring_step(1, 3)
+    ring_step(1, 4)
     share_on(6)
-    ring_step(1, 4)
     for copy in meta_in:
         copy.wait_recv()
     small = [
@@ -353,7 +364,7 @@
 
     preact = pre[...]
     sigma = jax.nn.sigmoid(preact)
-    paper_out[...] = (paper[...].astype(F32) + preact * sigma).astype(BF16)
+    outs[0] = (paper[...].astype(F32) + preact * sigma).astype(BF16)
     slope = sigma * (1.0 + preact * (1.0 - sigma))
     own = (cot[...].astype(F32) * slope).astype(BF16)
     grads[yc, 0] = own[0:block]
@@ -428,19 +439,27 @@
                 back[m, b, way, turns[b][way]].wait_recv()
                 total += back_recv[m, b, way, turns[b][way]].astype(F32)
             sums[m, x, pl.ds(b * block, block)] = total.astype(BF16)
-        sums_in[m] = gather_x(sums, sums_sem, m, None)
+        sums_in[m] = gather_x(sums, sums_sem, m)
     for m in range(2):
         chain_x(sums_in[m], sums, sums_sem, m)
-    for m, out in enumerate((paper_grad, author_grad)):
+    stores = [
+        pltpu.make_async_copy(outs.at[i], out, local_sem.at[i])
+        for i, out in enumerate((paper_out_hbm, paper_grad_hbm, author_grad_hbm))
+    ]
+    stores[0].start()
+    for m in range(2):
         end_x(sums_in[m])
         total = dot_right_flipped(sums[m, 0], rows[m, :, 0:quarter])
         for i in range(1, nx):
             total += dot_right_flipped(sums[m, i], rows[m, :, i * quarter : (i + 1) * quarter])
         if m == 0:
             total += pre[...]
-        out[...] = total.astype(BF16)
+        outs[1 + m] = total.astype(BF16)
+        stores[1 + m].start()
     for copy in sent:
         copy.wait_send()
+    for store in stores:
+        store.wait()
 
 
 def body(
@@ -473,7 +492,6 @@
         cite_owner, cite_source, cite_target, cite_edges, write_owner, write_author, write_paper, write_edges
     )
     steps = nz // 2 + 1
-    vmem = pl.BlockSpec(memory_space=pltpu.VMEM)
     hbm = pl.BlockSpec(memory_space=pl.ANY)
     unit = jax.ShapeDtypeStruct((n_rows, quarter), BF16)
 
@@ -483,9 +501,13 @@
     results = pl.pallas_call(
         functools.partial(kernel, nx, nyc, nz),
         out_shape=(unit, unit, unit),
-        in_specs=[pl.BlockSpec(memory_space=pltpu.SMEM)] + [vmem] * 11 + [hbm] * 5,
-        out_specs=(vmem, vmem, vmem),
+        in_specs=[pl.BlockSpec(memory_space=pltpu.SMEM)] + [hbm] * 16,
+        out_specs=(hbm, hbm, hbm),
         scratch_shapes=[
+            pltpu.VMEM((4, 1, cite_edges.shape[0]), jnp.int32),
+            pltpu.VMEM((4, 1, write_edges.shape[0]), jnp.int32),
+            pltpu.VMEM((n_rows, quarter), BF16),
+            pltpu.VMEM((3, n_rows, quarter), BF16),
             pltpu.VMEM(citation_weight_tiles.shape, BF16),
             pltpu.VMEM(authorship_weight_tiles.shape, BF16),
             pltpu.VMEM((3, width, quarter), BF16),
@@ -510,7 +532,7 @@
             pltpu.VMEM((2, 2, 2, steps, block, quarter), BF16),
             pltpu.VMEM((2, 2, 2, steps, block, quarter), BF16),
             pltpu.VMEM((2, nx, n_rows, quarter), BF16),
-            pltpu.SemaphoreType.DMA((9,)),
+            pltpu.SemaphoreType.DMA((20,)),
             sems(2, nx),
             sems(2, nyc),
             sems(2, nx, nyc),
@@ -542,15 +564,23 @@
         out_shape=(unit, unit, unit),
         in_specs=[hbm] * 3,
         out_specs=(hbm, hbm, hbm),
-        scratch_shapes=[pltpu.SemaphoreType.DMA((3,))],
+        scratch_shapes=[
+            pltpu.VMEM((3, n_rows, quarter), BF16),
+            pltpu.SemaphoreType.DMA((2, 3)),
+        ],
     )(*results)
 
 
 def hand_over(*refs):
-    copies = [pltpu.make_async_copy(refs[i], refs[3 + i], refs[6].at[i]) for i in range(3)]
-    for copy in copies:
+    sources, results, (held, sems) = refs[:3], refs[3:6], refs[6:]
+    ins = [pltpu.make_async_copy(sources[i], held.at[i], sems.at[0, i]) for i in range(3)]
+    ends = [pltpu.make_async_copy(held.at[i], results[i], sems.at[1, i]) for i in range(3)]
+    for copy in ins:
         copy.start()
-    for copy in copies:
+    for i in range(3):
+        ins[i].wait()
+        ends[i].start()
+    for copy in ends:
         copy.wait()
 
 

time: 122 us -> 104 us (0.85)
  Pallas kernels: 120 us -> 103 us
    pallas_call x1, Pallas kernels: 13 us -> 1.74 us  [body(): pl.pallas_call(hand_over, out_shape=(unit, unit, unit), in_specs=[hbm] *...]
    pallas_call x1, Pallas kernels: 107 us -> 101 us  [body(): pl.pallas_call(functools.partial(kernel, nx, nyc, nz), out_shape=(unit, u...]
where the time goes in v5:
time: 104 us
  Pallas kernels  103 us (99%)
  between operations  1.45 us (1%)
    pallas_call x1, Pallas kernels, body(): pl.pallas_call(functools.partial(kernel, nx, nyc, nz), out_shape=(unit, u...  101 us

profile of v5, /device:TPU:1, one launch (start us, length us, event | category | flops | bytes accessed | tf_op | source)
XLA Modules:
  0.0 104.2 jit_solution(7480845413714878883)
XLA Ops:
  1.3 101.0 %shard_map.184 = (bf16[256,256]{1,0:T(8,128)(2,1)}, bf16[256,256]{1,0:T(8,128)(2,1)}, bf16[256,256]{1,0:T(8,128)(2,1)}) custom-call(s32[1]{0:T(128)S(6)} %copy.20.cite_count, s32[1,48]{1,0:T(1,128)} %bitcast.8, s32[1,48]{1,0:T(1,128)} %bitcast.9, s32[1,48]{1,0:T(1,128)} %bitcast.10, s32[1,48]{1,0:T(1,128)} %bitcast.11, s32[1,32]{1,0:T(1,128)} %bitcast.12, ...), custom_call_target="tpu_custom_call" | custom-call | tf_op jit(solution)/shard_map/pallas_call | solution.py:501
  102.3 1.7 %shard_map.185 = (bf16[256,256]{1,0:T(8,128)(2,1)}, bf16[256,256]{1,0:T(8,128)(2,1)}, bf16[256,256]{1,0:T(8,128)(2,1)}) custom-call(bf16[256,256]{1,0:T(8,128)(2,1)} %get-tuple-element.6.refs_0_, bf16[256,256]{1,0:T(8,128)(2,1)} %get-tuple-element.7.refs_1_, bf16[256,256]{1,0:T(8,128)(2,1)} %get-tuple-element.8.refs_2_), custom_call_target="tpu_custom_call" | custom-call | tf_op jit(solution)/shard_map/pallas_call | solution.py:562

commit v6 on v5

--- a/solution.py
+++ b/solution.py
@@ -73,10 +73,12 @@
     part_send,
     part_recv,
     pre,
-    grads,
+    grads_left,
+    grads_right,
     grads_x,
     back_send,
     back_recv,
+    back_acc,
     sums,
     local_sem,
     feats_sem,
@@ -133,15 +135,15 @@
     def at_z(k):
         return (lax.rem(z + k + nz, nz) * nyc + yc, x)
 
-    def gather_x(buffer, sems, m):
-        piece = buffer.at[m, x]
-        return {k: send(piece, piece, sems, (m, k % nx), at_x(k)) for k in (1, -1)}
-
-    def chain_x(copies, buffer, sems, m):
+    def gather_x(buffer, sems, *at):
+        piece = buffer.at[at + (x,)]
+        return {k: send(piece, piece, sems, at + (k % nx,), at_x(k)) for k in (1, -1)}
+
+    def chain_x(copies, buffer, sems, *at):
         for b, onward in ((0, 1), (1, -1)):
             copies[onward].wait_recv()
-            piece = buffer.at[m, lax.rem(x - onward + nx, nx), pl.ds(b * block, block)]
-            copies[2 + b] = send(piece, piece, sems, (m, 2 * b), at_x(onward))
+            piece = buffer.at[at + (lax.rem(x - onward + nx, nx), pl.ds(b * block, block))]
+            copies[2 + b] = send(piece, piece, sems, at + (2 * b,), at_x(onward))
 
     def end_x(copies):
         for b in range(2):
@@ -344,85 +346,116 @@
                 (tiles_in if k == 0 else shared_in)[m, k, half].wait_recv()
         share_of(there(opposite[k]))
 
-    def pass_part(slot, device):
-        part_send[slot] = acc[...].astype(BF16)
-        part_in[slot] = send(part_send.at[slot], part_recv.at[slot], part_sem, (slot,), device)
+    cut = quarter // 2
+    halves = (slice(0, cut), slice(cut, quarter))
+
+    def pass_part(slot, h, device):
+        part_in[slot, h] = send(part_send.at[slot, h], part_recv.at[slot, h], part_sem, (slot, h), device)
 
     for k in range(ny):
         share_from(k)
-        pass_part(opposite[k], at_yc(0))
+        for h in range(2):
+            part_send[opposite[k], h] = acc[:, halves[h]].astype(BF16)
+            pass_part(opposite[k], h, at_yc(0))
     for k in range(ny, n_off):
         share_from(k)
-        part_in[opposite[k] - ny + 1].wait_recv()
-        acc[...] += part_recv[opposite[k] - ny + 1].astype(F32)
-        pass_part(opposite[k], at_yc(opposite[k]))
+        slot = opposite[k]
+        for h in range(2):
+            part_in[slot - ny + 1, h].wait_recv()
+            total = acc[:, halves[h]] + part_recv[slot - ny + 1, h].astype(F32)
+            part_send[slot, h] = total.astype(BF16)
+            if h == 0:
+                pass_part(slot, h, at_yc(slot))
+    for k in range(ny, n_off):
+        pass_part(opposite[k], 1, at_yc(opposite[k]))
     share_of(yc)
     pre[...] += acc[...]
-    for k in (0,) + tuple(range(ny, n_off)):
-        part_in[k].wait_recv()
-        pre[...] += part_recv[k].astype(F32)
-
-    preact = pre[...]
-    sigma = jax.nn.sigmoid(preact)
-    outs[0] = (paper[...].astype(F32) + preact * sigma).astype(BF16)
-    slope = sigma * (1.0 + preact * (1.0 - sigma))
-    own = (cot[...].astype(F32) * slope).astype(BF16)
-    grads[yc, 0] = own[0:block]
-    grads[yc, 1] = own[block:]
-    grads_x[x] = own
-    grads_in = {k: send(grads.at[yc], grads.at[yc], grads_sem, (k,), at_yc(k)) for k in range(ny, n_off)}
-    grads_in[0] = send(grads.at[yc], grads.at[yc], grads_sem, (0,), at_yc(0))
+
+    grads = (grads_left, grads_right)
+    grads_in = {}
+    for h in range(2):
+        preact = pre[:, halves[h]]
+        for k in (0,) + tuple(range(ny, n_off)):
+            part_in[k, h].wait_recv()
+            preact += part_recv[k, h].astype(F32)
+        sigma = jax.nn.sigmoid(preact)
+        slope = sigma * (1.0 + preact * (1.0 - sigma))
+        own = (cot[:, halves[h]].astype(F32) * slope).astype(BF16)
+        grads[h][yc, 0] = own[0:block]
+        grads[h][yc, 1] = own[block:]
+        for k in tuple(range(ny, n_off)) + (0,):
+            grads_in[h, k] = send(grads[h].at[yc], grads[h].at[yc], grads_sem, (h, k), at_yc(k))
+        grads_x[x, :, halves[h]] = own
+        outs[0, :, halves[h]] = (feats[0, x, :, halves[h]].astype(F32) + preact * sigma).astype(BF16)
     grads_x_in = [send(grads_x.at[x], grads_x.at[x], grads_x_sem, (k,), at_x(k)) for k in range(1, nx)]
-    for k in range(ny, n_off):
-        grads_in[k].wait_recv()
-        piece = grads.at[back_from(k)]
-        grads_in[k - ny + 1] = send(piece, piece, grads_sem, (k - ny + 1,), at_yc(0))
-
-    def back_of(m, place_z):
-        acc[...] = jnp.zeros_like(acc)
+
+    def grads_on(h):
+        for k in range(ny, n_off):
+            grads_in[h, k].wait_recv()
+            piece = grads[h].at[back_from(k)]
+            grads_in[h, k - ny + 1] = send(piece, piece, grads_sem, (h, k - ny + 1), at_yc(0))
+
+    def grads_end(h):
+        for k in range(ny):
+            grads_in[h, k].wait_recv()
+
+    def back_of(m, place_z, h):
+        back_acc[...] = jnp.zeros_like(back_acc)
 
         def step(i, carry):
             target = meta_is[i, place_z, 4 * m + 1]
-            product = dot_left_flipped(
-                tiles[m, i, place_z // 2, place_z % 2],
-                grads[i, target],
-            )
-            acc[0:block, :] += meta_fs[i, place_z, 4 * m + 2] * product
-            acc[block:, :] += meta_fs[i, place_z, 4 * m + 3] * product
+            product = dot_left_flipped(tiles[m, i, place_z // 2, place_z % 2], grads[h][i, target])
+            back_acc[0:block, :] += meta_fs[i, place_z, 4 * m + 2] * product
+            back_acc[block:, :] += meta_fs[i, place_z, 4 * m + 3] * product
             return carry
 
         lax.fori_loop(0, nyc, step, 0, unroll=UNROLL)
 
-    for k in range(ny):
-        grads_in[k].wait_recv()
     back = {}
 
-    def back_on(m, b, way, distance):
-        k = turns[b][way] - distance + 1
-        total = acc[b * block : (b + 1) * block, :]
-        if k > 1:
-            back[m, b, way, k - 1].wait_recv()
-            total += back_recv[m, b, way, k - 1].astype(F32)
-        back_send[m, b, way, k] = total.astype(BF16)
-        back[m, b, way, k] = send(
-            back_send.at[m, b, way, k],
-            back_recv.at[m, b, way, k],
-            back_sem,
-            (m, b, way, k),
-            at_z(1 if way == 0 else -1),
-        )
-
-    for distance in range(far, 0, -1):
+    def back_step(h, distance):
         for way in range(2):
+            if distance > turns[h][way]:
+                continue
+            sign = 1 if way == 0 else -1
+            k = turns[h][way] - distance + 1
             for m in range(2):
-                if distance < far:
-                    back_of(m, lax.rem(z + (distance if way == 0 else nz - distance), nz))
-                    for b in (way, 1 - way):
-                        back_on(m, b, way, distance)
-                elif way == 0:
-                    back_of(m, lax.rem(z + far, nz))
-                    back_on(m, 0, 0, far)
-                    back_on(m, 1, 1, far)
+                back_of(m, lax.rem(z + sign * distance + nz, nz), h)
+                total = back_acc[...]
+                if k > 1:
+                    back[m, h, way, k - 1].wait_recv()
+                    total += back_recv[m, h, way, k - 1].astype(F32)
+                back_send[m, h, way, k] = total.astype(BF16)
+                back[m, h, way, k] = send(
+                    back_send.at[m, h, way, k],
+                    back_recv.at[m, h, way, k],
+                    back_sem,
+                    (m, h, way, k),
+                    at_z(sign),
+                )
+
+    sums_in = {}
+
+    def back_end(h):
+        for m in range(2):
+            back_of(m, z, h)
+            total = back_acc[...]
+            for way in range(2):
+                back[m, h, way, turns[h][way]].wait_recv()
+                total += back_recv[m, h, way, turns[h][way]].astype(F32)
+            sums[m, h, x] = total.astype(BF16)
+            sums_in[m, h] = gather_x(sums, sums_sem, m, h)
+
+    grads_on(0)
+    grads_end(0)
+    back_step(0, far)
+    grads_on(1)
+    back_step(0, far - 1)
+    grads_end(1)
+    back_step(1, far)
+    for distance in range(far - 2, 0, -1):
+        back_step(0, distance)
+        back_step(1, distance + 1)
 
     for copy in grads_x_in:
         copy.wait_recv()
@@ -430,30 +463,31 @@
     for i in range(nx):
         total += dot_right_flipped(grads_x[i], rows[2, :, i * quarter : (i + 1) * quarter])
     pre[...] = total
-    sums_in = {}
+    back_end(0)
+    back_step(1, 1)
     for m in range(2):
-        back_of(m, z)
-        for b in range(2):
-            total = acc[b * block : (b + 1) * block, :]
-            for way in range(2):
-                back[m, b, way, turns[b][way]].wait_recv()
-                total += back_recv[m, b, way, turns[b][way]].astype(F32)
-            sums[m, x, pl.ds(b * block, block)] = total.astype(BF16)
-        sums_in[m] = gather_x(sums, sums_sem, m)
+        chain_x(sums_in[m, 0], sums, sums_sem, m, 0)
+    back_end(1)
     for m in range(2):
-        chain_x(sums_in[m], sums, sums_sem, m)
+        chain_x(sums_in[m, 1], sums, sums_sem, m, 1)
+
     stores = [
         pltpu.make_async_copy(outs.at[i], out, local_sem.at[i])
         for i, out in enumerate((paper_out_hbm, paper_grad_hbm, author_grad_hbm))
     ]
     stores[0].start()
+
+    def onto(m, h, total):
+        end_x(sums_in[m, h])
+        for i in range(nx):
+            first = i * quarter + h * cut
+            total += dot_right_flipped(sums[m, h, i], rows[m, :, first : first + cut])
+        return total
+
+    pre[...] = onto(0, 0, pre[...])
+    acc[...] = onto(1, 0, jnp.zeros_like(acc))
     for m in range(2):
-        end_x(sums_in[m])
-        total = dot_right_flipped(sums[m, 0], rows[m, :, 0:quarter])
-        for i in range(1, nx):
-            total += dot_right_flipped(sums[m, i], rows[m, :, i * quarter : (i + 1) * quarter])
-        if m == 0:
-            total += pre[...]
+        total = onto(m, 1, pre[...] if m == 0 else acc[...])
         outs[1 + m] = total.astype(BF16)
         stores[1 + m].start()
     for copy in sent:
@@ -524,25 +558,27 @@
             pltpu.SMEM((nyc, nz, 128), F32),
             pltpu.SMEM((nyc, nz, 128), jnp.int32),
             pltpu.VMEM((n_rows, quarter), F32),
-            pltpu.VMEM((nyc, n_rows, quarter), BF16),
-            pltpu.VMEM((nyc, n_rows, quarter), BF16),
+            pltpu.VMEM((nyc, 2, n_rows, quarter // 2), BF16),
+            pltpu.VMEM((nyc, 2, n_rows, quarter // 2), BF16),
             pltpu.VMEM((n_rows, quarter), F32),
-            pltpu.VMEM((nyc, 2, block, quarter), BF16),
+            pltpu.VMEM((nyc, 2, block, quarter // 2), BF16),
+            pltpu.VMEM((nyc, 2, block, quarter // 2), BF16),
             pltpu.VMEM((nx, n_rows, quarter), BF16),
-            pltpu.VMEM((2, 2, 2, steps, block, quarter), BF16),
-            pltpu.VMEM((2, 2, 2, steps, block, quarter), BF16),
-            pltpu.VMEM((2, nx, n_rows, quarter), BF16),
+            pltpu.VMEM((2, 2, 2, steps, n_rows, quarter // 2), BF16),
+            pltpu.VMEM((2, 2, 2, steps, n_rows, quarter // 2), BF16),
+            pltpu.VMEM((n_rows, quarter // 2), F32),
+            pltpu.VMEM((2, 2, nx, n_rows, quarter // 2), BF16),
             pltpu.SemaphoreType.DMA((20,)),
             sems(2, nx),
             sems(2, nyc),
             sems(2, nx, nyc),
             sems(2, 2, nyc),
             sems(2, 2, 2, steps),
-            sems(nyc),
-            sems(nyc),
+            sems(nyc, 2),
+            sems(2, nyc),
             sems(nx),
             sems(2, 2, 2, steps),
-            sems(2, nx),
+            sems(2, 2, nx),
         ],
         compiler_params=pltpu.CompilerParams(
             collective_id=0, has_side_effects=True, vmem_limit_bytes=56 * 1024 * 1024

time: 104 us -> 102 us (0.981); the launches traced: 104 us -> 100 us
  Pallas kernels: 103 us -> 98.9 us
    pallas_call x1, Pallas kernels: 101 us -> 97.1 us  [body(): pl.pallas_call(functools.partial(kernel, nx, nyc, nz), out_shape=(unit, u...]
where the time goes in v6:
time: 102 us; the launch traced here: 100 us
  Pallas kernels  98.9 us (97%)
  between operations  1.45 us (1%)
    pallas_call x1, Pallas kernels, body(): pl.pallas_call(functools.partial(kernel, nx, nyc, nz), out_shape=(unit, u...  97.1 us

profile of v6, /device:TPU:1, one launch (start us, length us, event | category | flops | bytes accessed | tf_op | source)
XLA Modules:
  0.0 100.3 jit_solution(10797949967225803235)
XLA Ops:
  1.3 97.1 %shard_map.184 = (bf16[256,256]{1,0:T(8,128)(2,1)}, bf16[256,256]{1,0:T(8,128)(2,1)}, bf16[256,256]{1,0:T(8,128)(2,1)}) custom-call(s32[1]{0:T(128)S(6)} %copy.20.cite_count, s32[1,48]{1,0:T(1,128)} %bitcast.8, s32[1,48]{1,0:T(1,128)} %bitcast.9, s32[1,48]{1,0:T(1,128)} %bitcast.10, s32[1,48]{1,0:T(1,128)} %bitcast.11, s32[1,32]{1,0:T(1,128)} %bitcast.12, ...), custom_call_target="tpu_custom_call" | custom-call | tf_op jit(solution)/shard_map/pallas_call | solution.py:535
  98.4 1.7 %shard_map.185 = (bf16[256,256]{1,0:T(8,128)(2,1)}, bf16[256,256]{1,0:T(8,128)(2,1)}, bf16[256,256]{1,0:T(8,128)(2,1)}) custom-call(bf16[256,256]{1,0:T(8,128)(2,1)} %get-tuple-element.6.refs_0_, bf16[256,256]{1,0:T(8,128)(2,1)} %get-tuple-element.7.refs_1_, bf16[256,256]{1,0:T(8,128)(2,1)} %get-tuple-element.8.refs_2_), custom_call_target="tpu_custom_call" | custom-call | tf_op jit(solution)/shard_map/pallas_call | solution.py:598

commit v7 on v6

--- a/solution.py
+++ b/solution.py
@@ -413,12 +413,12 @@
 
     back = {}
 
-    def back_step(h, distance):
-        for way in range(2):
-            if distance > turns[h][way]:
+    def back_step(h, k):
+        for way in (h, 1 - h):
+            if k > turns[h][way]:
                 continue
             sign = 1 if way == 0 else -1
-            k = turns[h][way] - distance + 1
+            distance = turns[h][way] - k + 1
             for m in range(2):
                 back_of(m, lax.rem(z + sign * distance + nz, nz), h)
                 total = back_acc[...]
@@ -448,14 +448,14 @@
 
     grads_on(0)
     grads_end(0)
+    back_step(0, 1)
+    grads_on(1)
+    grads_end(1)
+    back_step(1, 1)
+    for k in range(2, far):
+        back_step(0, k)
+        back_step(1, k)
     back_step(0, far)
-    grads_on(1)
-    back_step(0, far - 1)
-    grads_end(1)
-    back_step(1, far)
-    for distance in range(far - 2, 0, -1):
-        back_step(0, distance)
-        back_step(1, distance + 1)
 
     for copy in grads_x_in:
         copy.wait_recv()
@@ -463,8 +463,8 @@
     for i in range(nx):
         total += dot_right_flipped(grads_x[i], rows[2, :, i * quarter : (i + 1) * quarter])
     pre[...] = total
+    back_step(1, far)
     back_end(0)
-    back_step(1, 1)
     for m in range(2):
         chain_x(sums_in[m, 0], sums, sums_sem, m, 0)
     back_end(1)

time: 102 us -> 102 us (level)
  no operation moved by 1% of the time
where the time goes in v7:
time: 102 us; the launch traced here: 101 us
  Pallas kernels  99.5 us (98%)
  between operations  1.45 us (1%)
    pallas_call x1, Pallas kernels, body(): pl.pallas_call(functools.partial(kernel, nx, nyc, nz), out_shape=(unit, u...  97.8 us

profile of v7, /device:TPU:1, one launch (start us, length us, event | category | flops | bytes accessed | tf_op | source)
XLA Modules:
  0.0 101.0 jit_solution(11078912551625692240)
XLA Ops:
  1.3 97.8 %shard_map.184 = (bf16[256,256]{1,0:T(8,128)(2,1)}, bf16[256,256]{1,0:T(8,128)(2,1)}, bf16[256,256]{1,0:T(8,128)(2,1)}) custom-call(s32[1]{0:T(128)S(6)} %copy.20.cite_count, s32[1,48]{1,0:T(1,128)} %bitcast.8, s32[1,48]{1,0:T(1,128)} %bitcast.9, s32[1,48]{1,0:T(1,128)} %bitcast.10, s32[1,48]{1,0:T(1,128)} %bitcast.11, s32[1,32]{1,0:T(1,128)} %bitcast.12, ...), custom_call_target="tpu_custom_call" | custom-call | tf_op jit(solution)/shard_map/pallas_call | solution.py:535
  99.1 1.7 %shard_map.185 = (bf16[256,256]{1,0:T(8,128)(2,1)}, bf16[256,256]{1,0:T(8,128)(2,1)}, bf16[256,256]{1,0:T(8,128)(2,1)}) custom-call(bf16[256,256]{1,0:T(8,128)(2,1)} %get-tuple-element.6.refs_0_, bf16[256,256]{1,0:T(8,128)(2,1)} %get-tuple-element.7.refs_1_, bf16[256,256]{1,0:T(8,128)(2,1)} %get-tuple-element.8.refs_2_), custom_call_target="tpu_custom_call" | custom-call | tf_op jit(solution)/shard_map/pallas_call | solution.py:598

commit v8 on v7

--- a/solution.py
+++ b/solution.py
@@ -59,7 +59,9 @@
     win,
     rows,
     feats,
-    proj,
+    proj_cite,
+    proj_write,
+    shares,
     meta_f,
     meta_i,
     slot_tab,
@@ -250,10 +252,11 @@
     far = nz // 2
     turns = ((far, nz - 1 - far), (nz - 1 - far, far))
     ring = {}
+    proj = (proj_cite, proj_write)
 
     def pass_on(m, b, way, k):
         sign = 1 if way == 0 else -1
-        piece = proj.at[m, lax.rem(z - sign * (k - 1) + nz, nz), b]
+        piece = proj[m].at[lax.rem(z - sign * (k - 1) + nz, nz), b]
         ring[m, b, way, k] = send(piece, piece, proj_sem, (m, b, way, k), at_z(sign))
 
     def ring_step(m, k):
@@ -272,8 +275,8 @@
 
     def project_own(m):
         total = project(m, m).astype(BF16)
-        proj[m, z, 0] = total[0:block]
-        proj[m, z, 1] = total[block:]
+        proj[m][z, 0] = total[0:block]
+        proj[m][z, 1] = total[block:]
         ring_step(m, 1)
 
     for k in range(3):
@@ -316,35 +319,49 @@
         copy.start()
     for copy in small:
         copy.wait()
-    for m in range(2):
+    def ring_end(m):
         for b in range(2):
             for way in range(2):
                 ring[m, b, way, turns[b][way]].wait_recv()
 
-    def share_of(target):
+    def add_share(m, target):
+        def step(source_z, carry):
+            source = meta_is[target, source_z, 4 * m]
+            product = dot(tiles[m, target, source_z // 2, source_z % 2], proj[m][source_z, source])
+            acc[0:block, :] += meta_fs[target, source_z, 4 * m] * product
+            acc[block:, :] += meta_fs[target, source_z, 4 * m + 1] * product
+            return carry
+
+        lax.fori_loop(0, nz, step, 0, unroll=UNROLL)
+
+    part_in = {}
+
+    def share_wait(m, k):
+        for half in range(nx if k == 0 else 2):
+            (tiles_in if k == 0 else shared_in)[m, k, half].wait_recv()
+
+    def cite_share(k):
         acc[...] = jnp.zeros_like(acc)
-
-        def step(i, carry):
-            m = i // nz
-            s = i % nz
-            source = meta_is[target, s, 4 * m]
-            product = dot(
-                tiles[m, target, s // 2, s % 2],
-                proj[m, s, source],
-            )
-            acc[0:block, :] += meta_fs[target, s, 4 * m] * product
-            acc[block:, :] += meta_fs[target, s, 4 * m + 1] * product
-            return carry
-
-        lax.fori_loop(0, 2 * nz, step, 0, unroll=UNROLL)
-
-    part_in = {}
+        share_wait(0, k)
+        add_share(0, there(opposite[k]))
+
+    ring_end(0)
+    acc[...] = jnp.zeros_like(acc)
+    add_share(0, yc)
+    pre[...] += acc[...]
+    early = n_off - 1
+    for k in range(early):
+        cite_share(k)
+        shares[k] = acc[...]
+    ring_end(1)
 
     def share_from(k):
-        for m in range(2):
-            for half in range(nx if k == 0 else 2):
-                (tiles_in if k == 0 else shared_in)[m, k, half].wait_recv()
-        share_of(there(opposite[k]))
+        if k < early:
+            acc[...] = shares[k]
+        else:
+            cite_share(k)
+        share_wait(1, k)
+        add_share(1, there(opposite[k]))
 
     cut = quarter // 2
     halves = (slice(0, cut), slice(cut, quarter))
@@ -368,8 +385,9 @@
                 pass_part(slot, h, at_yc(slot))
     for k in range(ny, n_off):
         pass_part(opposite[k], 1, at_yc(opposite[k]))
-    share_of(yc)
-    pre[...] += acc[...]
+    acc[...] = pre[...]
+    add_share(1, yc)
+    pre[...] = acc[...]
 
     grads = (grads_left, grads_right)
     grads_in = {}
@@ -547,7 +565,9 @@
             pltpu.VMEM((3, width, quarter), BF16),
             pltpu.VMEM((3, quarter, width), BF16),
             pltpu.VMEM((2, nx, n_rows, quarter), BF16),
-            pltpu.VMEM((2, nz, 2, block, quarter), BF16),
+            pltpu.VMEM((nz, 2, block, quarter), BF16),
+            pltpu.VMEM((nz, 2, block, quarter), BF16),
+            pltpu.VMEM((nyc - 2, n_rows, quarter), F32),
             pltpu.VMEM((nyc, nz, 128), F32),
             pltpu.VMEM((nyc, nz, 128), jnp.int32),
             pltpu.SMEM((nyc, nz, 128), jnp.int32),

time: 102 us -> 102 us (level)
  no operation moved by 1% of the time
where the time goes in v8:
time: 102 us; the launch traced here: 101 us
  Pallas kernels  99.7 us (98%)
  between operations  1.45 us (1%)
    pallas_call x1, Pallas kernels, body(): pl.pallas_call(functools.partial(kernel, nx, nyc, nz), out_shape=(unit, u...  98 us

profile of v8, /device:TPU:1, one launch (start us, length us, event | category | flops | bytes accessed | tf_op | source)
XLA Modules:
  0.0 101.2 jit_solution(13886952209464846554)
XLA Ops:
  1.3 98.0 %shard_map.184 = (bf16[256,256]{1,0:T(8,128)(2,1)}, bf16[256,256]{1,0:T(8,128)(2,1)}, bf16[256,256]{1,0:T(8,128)(2,1)}) custom-call(s32[1]{0:T(128)S(6)} %copy.20.cite_count, s32[1,48]{1,0:T(1,128)} %bitcast.8, s32[1,48]{1,0:T(1,128)} %bitcast.9, s32[1,48]{1,0:T(1,128)} %bitcast.10, s32[1,48]{1,0:T(1,128)} %bitcast.11, s32[1,32]{1,0:T(1,128)} %bitcast.12, ...), custom_call_target="tpu_custom_call" | custom-call | tf_op jit(solution)/shard_map/pallas_call | solution.py:553
  99.3 1.7 %shard_map.185 = (bf16[256,256]{1,0:T(8,128)(2,1)}, bf16[256,256]{1,0:T(8,128)(2,1)}, bf16[256,256]{1,0:T(8,128)(2,1)}) custom-call(bf16[256,256]{1,0:T(8,128)(2,1)} %get-tuple-element.6.refs_0_, bf16[256,256]{1,0:T(8,128)(2,1)} %get-tuple-element.7.refs_1_, bf16[256,256]{1,0:T(8,128)(2,1)} %get-tuple-element.8.refs_2_), custom_call_target="tpu_custom_call" | custom-call | tf_op jit(solution)/shard_map/pallas_call | solution.py:618

commit v9 on v8

--- a/solution.py
+++ b/solution.py
@@ -293,22 +293,22 @@
     end_x(feats_y)
     project_own(1)
     tiles_out(6)
+    pre[...] = project(0, 2)
+    ring_step(0, 2)
     share_on(1)
+    ring_step(1, 2)
     share_on(2)
-    ring_step(0, 2)
-    ring_step(1, 2)
+    ring_step(0, 3)
     share_on(3)
-    pre[...] = project(0, 2)
+    ring_step(1, 3)
+    share_on(4)
+    ring_step(0, 4)
+    share_on(5)
+    ring_step(1, 4)
+    share_on(6)
     for m, source in enumerate((cite_tiles, write_tiles)):
         for j in range(nz):
             tiles[m, yc, j // 2, j % 2] = source[slot_tab[yc, j, 4 * m + 2]]
-    ring_step(0, 3)
-    ring_step(1, 3)
-    share_on(4)
-    share_on(5)
-    ring_step(0, 4)
-    ring_step(1, 4)
-    share_on(6)
     for copy in meta_in:
         copy.wait_recv()
     small = [

time: 102 us -> 102 us (level)
  no operation moved by 1% of the time
where the time goes in v9:
time: 102 us; the launch traced here: 101 us
  Pallas kernels  99.7 us (98%)
  between operations  1.45 us (1%)
    pallas_call x1, Pallas kernels, body(): pl.pallas_call(functools.partial(kernel, nx, nyc, nz), out_shape=(unit, u...  98 us

profile of v9, /device:TPU:1, one launch (start us, length us, event | category | flops | bytes accessed | tf_op | source)
XLA Modules:
  0.0 101.2 jit_solution(9699702186644978011)
XLA Ops:
  1.3 98.0 %shard_map.184 = (bf16[256,256]{1,0:T(8,128)(2,1)}, bf16[256,256]{1,0:T(8,128)(2,1)}, bf16[256,256]{1,0:T(8,128)(2,1)}) custom-call(s32[1]{0:T(128)S(6)} %copy.20.cite_count, s32[1,48]{1,0:T(1,128)} %bitcast.8, s32[1,48]{1,0:T(1,128)} %bitcast.9, s32[1,48]{1,0:T(1,128)} %bitcast.10, s32[1,48]{1,0:T(1,128)} %bitcast.11, s32[1,32]{1,0:T(1,128)} %bitcast.12, ...), custom_call_target="tpu_custom_call" | custom-call | tf_op jit(solution)/shard_map/pallas_call | solution.py:553
  99.3 1.7 %shard_map.185 = (bf16[256,256]{1,0:T(8,128)(2,1)}, bf16[256,256]{1,0:T(8,128)(2,1)}, bf16[256,256]{1,0:T(8,128)(2,1)}) custom-call(bf16[256,256]{1,0:T(8,128)(2,1)} %get-tuple-element.6.refs_0_, bf16[256,256]{1,0:T(8,128)(2,1)} %get-tuple-element.7.refs_1_, bf16[256,256]{1,0:T(8,128)(2,1)} %get-tuple-element.8.refs_2_), custom_call_target="tpu_custom_call" | custom-call | tf_op jit(solution)/shard_map/pallas_call | solution.py:618
